TPU v7x, 128 devices: a whole 4x4x4 slice. The times are simulated.
128 devices in a mesh: seq: 8 (over x, y_lo), tensor: 16 (over z, y_hi, core).
Axes of the slice: x: 4, y: 4 (y_hi: 2, y_lo: 2; y = y_hi * 2 + y_lo), z: 4, core: 2. Of those that a mesh axis runs over, the one named last changes fastest.
Arguments:
- inputs: bfloat16 [2048, 12288], P(('seq', 'tensor')), may hold values from -6 to 6
- out_grad: bfloat16 [2048, 12288], P(('seq', 'tensor')), may hold values from -0.59765625 to 0.59765625
- hidden_pre: bfloat16 [2048, 24576], P('seq', 'tensor'), may hold values from -8 to 8
- first_blocks: bfloat16 [4608, 128, 128], P('tensor'), may hold values from -0.078125 to 0.078125
- first_feat: int32 [4608], P('tensor'), may hold values from 0 to 95
- first_hid: int32 [4608], P('tensor'), may hold values from 0 to 191, as said below
- first_live: int32 [16], P('tensor'), may hold values from 144 to 288, as said below
- second_blocks: bfloat16 [4608, 128, 128], P('tensor'), may hold values from -0.109375 to 0.109375
- second_feat: int32 [4608], P('tensor'), may hold values from 0 to 95
- second_hid: int32 [4608], P('tensor'), may hold values from 0 to 191, as said below
- second_live: int32 [16], P('tensor'), may hold values from 144 to 288, as said below
Outputs:
- input_grad: bfloat16 [2048, 12288], P(('seq', 'tensor'))
- first_grad: bfloat16 [4608, 128, 128], P('tensor', 'seq')
- second_grad: bfloat16 [4608, 128, 128], P('tensor', 'seq')
Inputs may be any that keep to these rules, and one draw needn't show every extreme that they name: `first_hid`: slots of tensor index j name distinct block positions, with hidden blocks from j * 12 to (j + 1) * 12 - 1. `second_hid`: slots of tensor index j name distinct block positions, with hidden blocks from j * 12 to (j + 1) * 12 - 1. `first_live`: some index has all 288 slots live. `second_live`: some index has all 288 slots live.
All inputs are finite; a program needn't handle non-finite values.
Results may differ from a plain program's by a relative error of at most 0.023.
Values may be sent and summed in bfloat16 or wider, within the bound.
A program may use at most 256 MiB of HBM per device.

v0:
```python
import jax
import jax.numpy as jnp
from jax import lax
from jax.sharding import PartitionSpec as P

slope_coef = 0.7978845608028654
cubic_coef = 0.044715


def gelu_pair(values):
    inner_arg = slope_coef * (values + cubic_coef * values * values * values)
    tanh_part = jnp.tanh(inner_arg)
    output = 0.5 * values * (1.0 + tanh_part)
    slopes = 0.5 * (1.0 + tanh_part) + 0.5 * values * (1.0 - tanh_part * tanh_part) * slope_coef * (
        1.0 + 3.0 * cubic_coef * values * values
    )
    return (output, slopes)


def place_blocks(pieces, onehot):
    upper = pieces.astype(jnp.bfloat16)
    lower = (pieces - upper.astype(jnp.float32)).astype(jnp.bfloat16)
    table = onehot.astype(jnp.bfloat16)
    first_sum = jnp.einsum("tbf,bk->tkf", upper, table, preferred_element_type=jnp.float32)
    second_sum = jnp.einsum("tbf,bk->tkf", lower, table, preferred_element_type=jnp.float32)
    return first_sum + second_sum


def shards(
    inputs,
    out_grad,
    hidden_pre,
    first_blocks,
    first_feat,
    first_hid,
    first_live,
    second_blocks,
    second_feat,
    second_hid,
    second_live,
):
    block_size = first_blocks.shape[1]
    slots = first_blocks.shape[0]
    hid_count = hidden_pre.shape[1] // block_size
    whole_in = lax.all_gather(inputs, "tensor", axis=0, tiled=True)
    whole_grad = lax.all_gather(out_grad, "tensor", axis=0, tiled=True)
    row_count = whole_in.shape[0]
    feat_count = whole_in.shape[1] // block_size
    hid_base = lax.axis_index("tensor") * hid_count
    local_one = first_hid - hid_base
    local_two = second_hid - hid_base
    slot_order = jnp.arange(slots, dtype=jnp.int32)
    alive_one = slot_order < first_live[0]
    alive_two = slot_order < second_live[0]
    values, slopes = gelu_pair(hidden_pre.astype(jnp.float32))
    activation = values.astype(jnp.bfloat16).reshape(row_count, hid_count, block_size)
    grad_tiles = whole_grad.reshape(row_count, feat_count, block_size)
    in_tiles = whole_in.reshape(row_count, feat_count, block_size)
    hidden_ids = jnp.arange(hid_count, dtype=jnp.int32)
    feature_ids = jnp.arange(feat_count, dtype=jnp.int32)
    blocks = second_blocks
    feature_idx = second_feat
    hidden_idx = local_two
    alive_mask = alive_two
    grad_cols = jnp.take(grad_tiles, feature_idx, axis=1)
    contrib = jnp.einsum("tbf,bhf->tbh", grad_cols, blocks, preferred_element_type=jnp.float32)
    onehot = (hidden_idx[:, None] == hidden_ids[None, :]) & alive_mask[:, None]
    hidden_sum = place_blocks(contrib, onehot)
    act_cols = jnp.take(activation, hidden_idx, axis=1)
    weight_part = jnp.einsum(
        "tbh,tbf->bhf", act_cols, grad_cols, preferred_element_type=jnp.float32
    )
    grad_two = jnp.where(alive_mask[:, None, None], weight_part, 0.0)
    pre_grad = (hidden_sum.reshape(row_count, hid_count * block_size) * slopes).astype(jnp.bfloat16)
    pre_tiles = pre_grad.reshape(row_count, hid_count, block_size)
    blocks = first_blocks
    feature_idx = first_feat
    hidden_idx = local_one
    alive_mask = alive_one
    pre_cols = jnp.take(pre_tiles, hidden_idx, axis=1)
    back = jnp.einsum("tbh,bfh->tbf", pre_cols, blocks, preferred_element_type=jnp.float32)
    onehot = (feature_idx[:, None] == feature_ids[None, :]) & alive_mask[:, None]
    total_sum = place_blocks(back, onehot)
    input_grad = lax.psum_scatter(
        total_sum.reshape(
            lax.axis_size("tensor") * (row_count // lax.axis_size("tensor")),
            feat_count * block_size,
        ).astype(jnp.bfloat16),
        "tensor",
        scatter_dimension=0,
        tiled=True,
    )
    feature_idx = first_feat
    hidden_idx = local_one
    alive_mask = alive_one
    in_cols = jnp.take(in_tiles, feature_idx, axis=1)
    pre_cols = jnp.take(pre_tiles, hidden_idx, axis=1)
    weight_part = jnp.einsum("tbf,tbh->bfh", in_cols, pre_cols, preferred_element_type=jnp.float32)
    grad_one = jnp.where(alive_mask[:, None, None], weight_part, 0.0)
    summed_one, summed_two = (
        lax.psum_scatter(
            grad_one.astype(jnp.bfloat16), "seq", scatter_dimension=1, tiled=True
        ).astype(jnp.float32),
        lax.psum_scatter(
            grad_two.astype(jnp.bfloat16), "seq", scatter_dimension=1, tiled=True
        ).astype(jnp.float32),
    )
    return (input_grad, summed_one.astype(jnp.bfloat16), summed_two.astype(jnp.bfloat16))


def solution(mesh):
    in_specs = (
        P(("seq", "tensor"), None),
        P(("seq", "tensor"), None),
        P("seq", "tensor"),
        P("tensor", None, None),
        P("tensor"),
        P("tensor"),
        P("tensor"),
        P("tensor", None, None),
        P("tensor"),
        P("tensor"),
        P("tensor"),
    )
    out_specs = (P(("seq", "tensor"), None), P("tensor", "seq", None), P("tensor", "seq", None))
    return jax.shard_map(shards, mesh=mesh, in_specs=in_specs, out_specs=out_specs, check_vma=False)
```

profile of v0, /device:TPU:1, one launch (start us, length us, event | category | flops | bytes accessed | tf_op | source)
XLA Modules:
  0.0 762.6 jit_solution(507706903035126535)
XLA Ops:
  14.0 64.4 %all-gather.3.cloned.1.call-done = bf16[256,12288]{1,0:T(8,128)(2,1)} async-done(((bf16[16,12288]{1,0:T(8,128)(2,1)}), bf16[256,12288]{1,0:T(8,128)(2,1)}) %all-gather.3.cloned.1.call-update) | async-done | bytes 6291472 | tf_op jit(solution)/shard_map/all_gather | solution.py:46
  78.4 8.6 %copy.42 = bf16[256,12288]{0,1:T(8,128)(2,1)} copy(bf16[256,12288]{1,0:T(8,128)(2,1)} %all-gather.3.cloned.1.call-done) | data formatting | bytes 12582912 | tf_op jit(solution)/shard_map/all_gather | solution.py:46
  87.0 8.8 %copy.43 = bf16[256,96,128]{2,0,1:T(8,128)(2,1)} copy(bf16[256,96,128]{0,2,1:T(8,128)(2,1)} %bitcast.69) | data formatting | bytes 12582912 | tf_op jit(solution)/shard_map/reshape | solution.py:57
  95.8 13.5 %gather_fusion = bf16[288,256,128]{2,1,0:T(8,128)(2,1)} fusion(bf16[256,96,128]{2,0,1:T(8,128)(2,1)} %copy.43, s32[1024]{0:T(1024)S(1)} %pad_clamp_fusion.3), kind=kCustom, calls=%fused_computation.clone | custom fusion | bytes 37749888 | tf_op jit(solution)/shard_map/jit(_take)/gather | solution.py:65
  109.3 28.5 %fusion.1 = (bf16[256,288,128]{2,0,1:T(8,128)(2,1)}, bf16[256,288,128]{2,0,1:T(8,128)(2,1)}) fusion(bf16[288,128,128]{2,1,0:T(8,128)(2,1)} %param.22, bf16[288,256,128]{2,1,0:T(8,128)(2,1)} %gather_fusion, pred[288]{0:T(512)(128)(4,1)S(1)} %get-tuple-element.18), kind=kOutput, calls=%fused_computation.9 | convolution fusion | flops 2463105024 | bytes 66060576 | tf_op jit(solution)/shard_map/tbf,bhf->tbh/dot_general | solution.py:66
  137.8 19.0 %fusion.16 = f32[12,256,128]{2,0,1:T(8,128)S(1)} fusion(bf16[256,288,128]{2,0,1:T(8,128)(2,1)} %get-tuple-element.11, s32[288]{0:T(512)S(1)} %get-tuple-element.6, pred[288]{0:T(512)(128)(4,1)S(1)} %get-tuple-element.17), kind=kOutput, calls=%fused_computation.24 | convolution fusion | flops 226499328 | bytes 20448672 | tf_op jit(solution)/shard_map/tbf,bk->tkf/dot_general | solution.py:25
  156.8 18.8 %add_bitcast_fusion = f32[256,12,128]{2,1,0:T(8,128)S(1)} fusion(f32[12,256,128]{2,0,1:T(8,128)S(1)} %fusion.16, bf16[256,288,128]{2,0,1:T(8,128)(2,1)} %get-tuple-element.12, s32[288]{0:T(512)S(1)} %get-tuple-element.6, pred[288]{0:T(512)(128)(4,1)S(1)} %get-tuple-element.17), kind=kOutput, calls=%fused_computation.47 | convolution fusion | flops 226892544 | bytes 22021536 | tf_op jit(solution)/shard_map/tbf,bk->tkf/dot_general | solution.py:24
  175.7 1.7 copy.46
  177.3 3.4 fusion.43
  180.8 1.5 copy.48
  182.3 10.8 %gather_fusion.1 = bf16[288,256,128]{2,1,0:T(8,128)(2,1)} fusion(bf16[256,12,128]{2,0,1:T(8,128)(2,1)S(1)} %copy.48, s32[1024]{0:T(1024)S(1)} %pad_clamp_fusion.2), kind=kCustom, calls=%fused_computation.1.clone | custom fusion | bytes 37749888 | tf_op jit(solution)/shard_map/jit(_take)/gather | solution.py:80
  193.1 37.3 %fusion = (bf16[256,288,128]{2,0,1:T(8,128)(2,1)}, bf16[256,288,128]{2,0,1:T(8,128)(2,1)}) fusion(bf16[288,128,128]{2,1,0:T(8,128)(2,1)} %param.18, bf16[288,256,128]{2,1,0:T(8,128)(2,1)} %gather_fusion.1, pred[288]{0:T(512)(128)(4,1)S(1)} %get-tuple-element.15), kind=kOutput, calls=%fused_computation.6 | convolution fusion | flops 2463105024 | bytes 66060576 | tf_op jit(solution)/shard_map/tbh,bfh->tbf/dot_general | solution.py:81
  230.4 22.6 %fusion.12 = f32[96,256,128]{2,0,1:T(8,128)} fusion(bf16[256,288,128]{2,0,1:T(8,128)(2,1)} %get-tuple-element.7, s32[288]{0:T(512)S(1)} %copy-done, pred[288]{0:T(512)(128)(4,1)S(1)} %iota_compare_fusion.3), kind=kOutput, calls=%fused_computation.20 | convolution fusion | flops 1811994624 | bytes 31458720 | tf_op jit(solution)/shard_map/tbf,bk->tkf/dot_general | solution.py:25
  253.0 24.2 %add_convert_fusion = bf16[96,256,128]{2,0,1:T(8,128)(2,1)} fusion(f32[96,256,128]{2,0,1:T(8,128)} %fusion.12, bf16[256,288,128]{2,0,1:T(8,128)(2,1)} %get-tuple-element.8, s32[288]{0:T(512)S(1)} %copy-done, pred[288]{0:T(512)(128)(4,1)S(1)} %iota_compare_fusion.3), kind=kOutput, calls=%fused_computation.36 | convolution fusion | flops 1818286080 | bytes 37750176 | tf_op jit(solution)/shard_map/tbf,bk->tkf/dot_general | solution.py:24
  277.2 8.4 %copy.72 = bf16[32,8,96,128]{3,1,2,0:T(8,128)(2,1)} copy(bf16[32,8,96,128]{3,2,1,0:T(8,128)(2,1)} %bitcast.67) | data formatting | bytes 12582912
  285.8 9.0 %copy.51 = bf16[256,12288]{0,1:T(8,128)(2,1)} copy(bf16[256,12288]{1,0:T(8,128)(2,1)} %all-gather.5.cloned.1.call-done) | data formatting | bytes 12582912 | tf_op jit(solution)/shard_map/all_gather | solution.py:45
  294.8 8.9 %copy.52 = bf16[256,96,128]{2,0,1:T(8,128)(2,1)} copy(bf16[256,96,128]{0,2,1:T(8,128)(2,1)} %bitcast.70) | data formatting | bytes 12582912 | tf_op jit(solution)/shard_map/reshape | solution.py:58
  303.7 14.0 %gather_fusion.2 = bf16[288,256,128]{2,1,0:T(8,128)(2,1)} fusion(bf16[256,96,128]{2,0,1:T(8,128)(2,1)} %copy.52, s32[1024]{0:T(1024)S(1)} %pad_clamp_fusion.1), kind=kCustom, calls=%fused_computation.2.clone | custom fusion | bytes 37749888 | tf_op jit(solution)/shard_map/jit(_take)/gather | solution.py:96
  317.6 20.0 %select_convert_fusion.1 = bf16[288,128,128]{2,1,0:T(8,128)(2,1)} fusion(pred[288]{0:T(512)(128)(4,1)S(1)} %iota_compare_fusion.3, bf16[288,256,128]{2,1,0:T(8,128)(2,1)} %gather_fusion.1, pred[288]{0:T(512)(128)(4,1)S(1)} %get-tuple-element.15, bf16[288,256,128]{2,1,0:T(8,128)(2,1)} %gather_fusion.2, pred[288]{0:T(512)(128)(4,1)S(1)} %compare_and_fusion.1), kind=kOutput, calls=%fused_computation.31 | convolution fusion | flops 2444230656 | bytes 47186784 | tf_op jit(solution)/shard_map/tbf,tbh->bfh/dot_general | solution.py:98
  338.1 10.8 %gather_fusion.3 = bf16[288,256,128]{2,1,0:T(8,128)(2,1)} fusion(bf16[256,12,128]{2,0,1:T(8,128)(2,1)S(1)} %copy.54, s32[1024]{0:T(1024)S(1)} %pad_clamp_fusion), kind=kCustom, calls=%fused_computation.3.clone | custom fusion | bytes 37749888 | tf_op jit(solution)/shard_map/jit(_take)/gather | solution.py:69
  349.0 19.8 %select_convert_fusion = bf16[288,128,128]{2,1,0:T(8,128)(2,1)} fusion(pred[288]{0:T(512)(128)(4,1)S(1)} %get-tuple-element.17, bf16[288,256,128]{2,1,0:T(8,128)(2,1)} %gather_fusion, pred[288]{0:T(512)(128)(4,1)S(1)} %get-tuple-element.18, bf16[288,256,128]{2,1,0:T(8,128)(2,1)} %gather_fusion.3, pred[288]{0:T(512)(128)(4,1)S(1)} %copy-done.1), kind=kOutput, calls=%fused_computation.30 | convolution fusion | flops 2444230656 | bytes 47186784 | tf_op jit(solution)/shard_map/tbh,tbf->bhf/dot_general | solution.py:70
  368.8 2.2 reduce-scatter.4.cloned.1.call-done
  370.9 191.8 %reduce-scatter.6.cloned.1.call-done = bf16[288,16,128]{2,1,0:T(8,128)(2,1)} async-done(((bf16[288,128,128]{2,1,0:T(8,128)(2,1)}), bf16[288,16,128]{2,1,0:T(8,128)(2,1)}) %reduce-scatter.6.cloned.1.call-update) | async-done | bytes 1179664 | tf_op jit(solution)/shard_map/reduce_scatter | solution.py:101
  562.8 192.8 %reduce-scatter.8.cloned.1.call-done = bf16[288,16,128]{2,1,0:T(8,128)(2,1)} async-done(((bf16[288,128,128]{2,1,0:T(8,128)(2,1)}), bf16[288,16,128]{2,1,0:T(8,128)(2,1)}) %reduce-scatter.8.cloned.1.call-update) | async-done | bytes 1179664 | tf_op jit(solution)/shard_map/reduce_scatter | solution.py:104
  (28 shorter events, 6.1 us)
Async XLA Ops:
  7.2 71.2 %all-gather.3.cloned.1.call-start = ((), (), s32[]{:S(2)}) async-start(), calls=%async_computation.3 | async-start | bytes 6684672 | tf_op jit(solution)/shard_map/all_gather | solution.py:46
  7.9 277.8 %all-gather.5.cloned.1.call-start = ((), (), s32[]{:S(2)}) async-start(), calls=%async_computation.5 | async-start | bytes 6684672 | tf_op jit(solution)/shard_map/all_gather | solution.py:45
  8.6 362.3 %reduce-scatter.4.cloned.1.call-start = ((), (), s32[]{:S(2)}) async-start(), calls=%async_computation.4 | async-start | bytes 6684672 | tf_op jit(solution)/shard_map/reduce_scatter | solution.py:84
  193.1 37.3 %copy-start = (s32[288]{0:T(512)S(1)}, s32[288]{0:T(512)}, u32[]{:S(2)}) copy-start(s32[288]{0:T(512)} %param.19) | copy-start | bytes 3460
  285.6 277.1 %reduce-scatter.6.cloned.1.call-start = ((), (), s32[]{:S(2)}) async-start(), calls=%async_computation.6 | async-start | bytes 10616832 | tf_op jit(solution)/shard_map/reduce_scatter | solution.py:101
  337.7 417.9 %reduce-scatter.8.cloned.1.call-start = ((), (), s32[]{:S(2)}) async-start(), calls=%async_computation.7 | async-start | bytes 10616832 | tf_op jit(solution)/shard_map/reduce_scatter | solution.py:104
  338.1 10.8 %copy-start.1 = (pred[288]{0:T(512)(128)(4,1)S(1)}, pred[288]{0:T(512)(128)(4,1)}, u32[]{:S(2)}) copy-start(pred[288]{0:T(512)(128)(4,1)} %get-tuple-element.5) | copy-start | bytes 868
Sparse Core Ops, SparseCore 0:
  10.5 67.8 all-gather.2
  80.8 61.9 all-gather.4
  285.8 85.1 reduce-scatter.3
  373.9 188.7 reduce-scatter.5
  565.7 189.8 reduce-scatter.7
where the time goes:
time: 768 us; the launch traced here: 763 us
  waiting for transfers between devices  453 us (59%)
  matrix products  190 us (25%)
  local copies, waits for them, and re-layouts  97.7 us (13%)
  between operations  15.6 us (2%)
    reduce_scatter x1, waiting for transfers between devices, shards(): lax.psum_scatter(grad_two.astype(jnp.bfloat16), 'seq', scatter_dimension=...  193 us
    reduce_scatter x1, waiting for transfers between devices, shards(): lax.psum_scatter(grad_one.astype(jnp.bfloat16), 'seq', scatter_dimension=...  192 us
    all_gather x1, waiting for transfers between devices, shards(): whole_grad = lax.all_gather(out_grad, 'tensor', axis=0, tiled=True)  64.4 us
    dot_general x2, matrix products, place_blocks(): jnp.einsum('tbf,bk->tkf', upper, table, preferred_element_type=jnp.float32)  43 us
    dot_general x2, matrix products, place_blocks(): jnp.einsum('tbf,bk->tkf', lower, table, preferred_element_type=jnp.float32)  41.7 us
    dot_general x1, matrix products, shards(): jnp.einsum('tbh,bfh->tbf', pre_cols, blocks, preferred_element_type=jnp.f...  37.3 us
    dot_general x1, matrix products, shards(): jnp.einsum('tbf,bhf->tbh', grad_cols, blocks, preferred_element_type=jnp....  28.5 us
    dot_general x1, matrix products, shards(): jnp.einsum('tbf,tbh->bfh', in_cols, pre_cols, preferred_element_type=jnp....  20 us
  transfers between devices with their start and end apart: 5, of which 4 were waited for; matrix products, arithmetic and copies ran while one was open for 39% of the time, Pallas kernels for 0%

commit v1 on v0

v1 whole, which is shorter than its diff:
```python
import functools

import jax
import jax.numpy as jnp
from jax import lax
from jax.experimental import pallas as pl
from jax.experimental.pallas import tpu as pltpu
from jax.sharding import PartitionSpec as P

MESH = pl.DeviceIdType.MESH
BF = jnp.bfloat16
F32 = jnp.float32
ANY = pl.BlockSpec(memory_space=pl.ANY)
SMEM = pl.BlockSpec(memory_space=pltpu.SMEM)
VMEM = pl.BlockSpec(memory_space=pltpu.VMEM)
MIB = 1024 * 1024

slope_coef = 0.7978845608028654
cubic_coef = 0.044715


def gelu_value(p):
    th = jnp.tanh(slope_coef * (p + cubic_coef * p * p * p))
    return 0.5 * p * (1.0 + th)


def gelu_slope(p):
    th = jnp.tanh(slope_coef * (p + cubic_coef * p * p * p))
    return 0.5 * (1.0 + th) + 0.5 * p * (1.0 - th * th) * slope_coef * (1.0 + 3.0 * cubic_coef * p * p)


class Here:
    def __init__(self):
        s = lax.axis_index("seq")
        t = lax.axis_index("tensor")
        self.s, self.t = s, t
        self.x, self.yl = s // 2, s % 2
        self.z, self.yh, self.c = t // 4, (t // 2) % 2, t % 2

    def dev(self, dx=0, fl=0, dz=0, fh=0, fc=0):
        x = (self.x + dx) % 4
        z = (self.z + dz) % 4
        yl = (self.yl + fl) % 2
        yh = (self.yh + fh) % 2
        c = (self.c + fc) % 2
        return (x * 2 + yl, z * 4 + yh * 2 + c)


class Copies:
    def __init__(self, send, recv):
        self.send_sems, self.recv_sems = send, recv
        self.sent = []

    def send(self, i, src, dst, device):
        copy = pltpu.make_async_remote_copy(
            src_ref=src,
            dst_ref=dst,
            send_sem=self.send_sems.at[i],
            recv_sem=self.recv_sems.at[i],
            device_id=device,
            device_id_type=MESH,
        )
        copy.start()
        self.sent.append(copy)

    def arrived(self, i, dst, device):
        pltpu.make_async_remote_copy(
            src_ref=dst,
            dst_ref=dst,
            send_sem=self.send_sems.at[i],
            recv_sem=self.recv_sems.at[i],
            device_id=device,
            device_id_type=MESH,
        ).wait_recv()

    def drain(self):
        for copy in self.sent:
            copy.wait_send()


def greet(devices):
    barrier = pltpu.get_barrier_semaphore()
    for device in devices:
        pl.semaphore_signal(barrier, inc=1, device_id=device, device_id_type=MESH)
    pl.semaphore_wait(barrier, len(devices))


class TensorGather:
    def __init__(self, me, copies, base, own, slot):
        self.me, self.k, self.b, self.own, self.slot = me, copies, base, own, slot

    def at(self, dz, fh, fc=0):
        me = self.me
        return self.slot(((me.z + dz) % 4) * 4 + ((me.yh + fh) % 2) * 2 + (me.c + fc) % 2)

    def start(self):
        me, k, b, mine = self.me, self.k, self.b, self.at(0, 0)
        k.send(b + 1, self.own, mine, me.dev(fh=1))
        k.send(b + 2, self.own, mine, me.dev(dz=1))
        k.send(b + 3, self.own, mine, me.dev(dz=-1))
        k.send(b + 0, self.own, mine, me.dev(fc=1))

    def spread(self):
        me, k, b = self.me, self.k, self.b
        core = me.dev(fc=1)
        got = self.at(0, 1)
        k.arrived(b + 1, got, me.dev(fh=1))
        k.send(b + 4, got, got, me.dev(dz=1))
        k.send(b + 5, got, got, me.dev(dz=-1))
        k.send(b + 8, got, got, core)
        got = self.at(-1, 0)
        k.arrived(b + 2, got, me.dev(dz=-1))
        k.send(b + 6, got, got, me.dev(dz=1))
        k.send(b + 9, got, got, core)
        got = self.at(1, 0)
        k.arrived(b + 3, got, me.dev(dz=1))
        k.send(b + 11, got, got, core)
        got = self.at(1, 1)
        k.arrived(b + 5, got, me.dev(dz=1))
        k.send(b + 7, got, got, me.dev(dz=-1))
        k.send(b + 12, got, got, core)
        got = self.at(-1, 1)
        k.arrived(b + 4, got, me.dev(dz=-1))
        k.send(b + 10, got, got, core)

    def finish(self):
        me, k, b = self.me, self.k, self.b
        core = me.dev(fc=1)
        got = self.at(2, 0)
        k.arrived(b + 6, got, me.dev(dz=-1))
        k.send(b + 13, got, got, core)
        got = self.at(2, 1)
        k.arrived(b + 7, got, me.dev(dz=1))
        k.send(b + 14, got, got, core)
        for i, dz, fh in ((0, 0, 0), (8, 0, 1), (9, -1, 0), (10, -1, 1), (11, 1, 0), (12, 1, 1), (13, 2, 0), (14, 2, 1)):
            k.arrived(b + i, self.at(dz, fh, 1), core)


class RowGather:
    def __init__(self, me, copies, base, own, slots):
        self.me, self.k, self.b, self.own, self.slots = me, copies, base, own, slots
        self.half = own.shape[0] // 2

    def start(self):
        me, k, b = self.me, self.k, self.b
        k.send(b + 0, self.own, self.slots.at[me.x], me.dev(dx=1))
        k.send(b + 1, self.own, self.slots.at[me.x], me.dev(dx=-1))

    def spread(self):
        me, k, b, half = self.me, self.k, self.b, self.half
        left, right = (me.x + 3) % 4, (me.x + 1) % 4
        k.arrived(b + 0, self.slots.at[left], me.dev(dx=-1))
        part = self.slots.at[left, pl.ds(0, half)]
        k.send(b + 2, part, part, me.dev(dx=1))
        k.arrived(b + 1, self.slots.at[right], me.dev(dx=1))
        part = self.slots.at[right, pl.ds(half, half)]
        k.send(b + 3, part, part, me.dev(dx=-1))

    def finish(self):
        me, k, b, half = self.me, self.k, self.b, self.half
        far = (me.x + 2) % 4
        k.arrived(b + 2, self.slots.at[far, pl.ds(0, half)], me.dev(dx=-1))
        k.arrived(b + 3, self.slots.at[far, pl.ds(half, half)], me.dev(dx=1))


def gather_one(grad, acts, in_cut, grad_cut, all_grad, all_acts, in_x, grad_x, send, recv, local):
    me = Here()
    greet([me.dev(fc=1), me.dev(fh=1), me.dev(dz=1), me.dev(dz=-1), me.dev(dx=1), me.dev(dx=-1), me.dev(dx=2)])
    k = Copies(send, recv)
    rows = TensorGather(me, k, 0, grad, lambda t: all_grad.at[t])
    cols = RowGather(me, k, 15, acts, all_acts)
    rows.start()
    for i, dx in enumerate((1, 2, 3)):
        to = (me.x + dx) % 4
        k.send(19 + i, grad_cut.at[to], grad_x.at[me.x], me.dev(dx=dx))
        k.send(22 + i, in_cut.at[to], in_x.at[me.x], me.dev(dx=dx))
    cols.start()
    own = [
        pltpu.make_async_copy(grad, all_grad.at[me.t], local.at[0]),
        pltpu.make_async_copy(acts, all_acts.at[me.x], local.at[1]),
        pltpu.make_async_copy(grad_cut.at[me.x], grad_x.at[me.x], local.at[2]),
        pltpu.make_async_copy(in_cut.at[me.x], in_x.at[me.x], local.at[3]),
    ]
    for copy in own:
        copy.start()
    rows.spread()
    cols.spread()
    rows.finish()
    cols.finish()
    for i, dx in enumerate((1, 2, 3)):
        src = (me.x + 4 - dx) % 4
        k.arrived(19 + i, grad_x.at[src], me.dev(dx=-dx))
        k.arrived(22 + i, in_x.at[src], me.dev(dx=-dx))
    k.drain()
    for copy in own:
        copy.wait()


def gather_two(pre, in_x, grad_x, all_pre, in_all, grad_all, send, recv, local):
    me = Here()
    greet([me.dev(fc=1), me.dev(fh=1), me.dev(dz=1), me.dev(dz=-1), me.dev(dx=1), me.dev(dx=-1)])
    k = Copies(send, recv)
    one = TensorGather(me, k, 0, grad_x, lambda t: grad_all.at[:, t])
    two = TensorGather(me, k, 15, in_x, lambda t: in_all.at[:, t])
    cols = RowGather(me, k, 30, pre, all_pre)
    cols.start()
    one.start()
    two.start()
    own = [
        pltpu.make_async_copy(pre, all_pre.at[me.x], local.at[0]),
        pltpu.make_async_copy(grad_x, grad_all.at[:, me.t], local.at[1]),
        pltpu.make_async_copy(in_x, in_all.at[:, me.t], local.at[2]),
    ]
    for copy in own:
        copy.start()
    one.spread()
    cols.spread()
    two.spread()
    one.finish()
    two.finish()
    cols.finish()
    k.drain()
    for copy in own:
        copy.wait()


def blocks_at(blocks, table, rows, cols, width):
    return jnp.concatenate(
        [jnp.concatenate([blocks[table[r * width + j]] for j in cols], axis=1) for r in rows], axis=0
    )


def load_blocks(blocks, held, sem):
    copy = pltpu.make_async_copy(blocks, held.at[pl.ds(0, blocks.shape[0])], sem)
    copy.start()
    held[blocks.shape[0]] = jnp.zeros(held.shape[1:], held.dtype)
    copy.wait()


NT = (((1,), (1,)), ((), ()))
TN = (((0,), (0,)), ((), ()))


def pre_kernel(table, grad, blocks, hidden, out, held, acc, sem):
    k = pl.program_id(0)

    @pl.when(k == 0)
    def _():
        load_blocks(blocks, held, sem)

    acc[...] = jnp.zeros_like(acc)

    def step(i, _):
        j = i * 8
        w = blocks_at(held, table, (2 * k, 2 * k + 1), [j + a for a in range(8)], 96)
        left = grad[:, pl.ds(pl.multiple_of(j * 128, 1024), 1024)]
        acc[...] += lax.dot_general(left, w, NT, preferred_element_type=F32)
        return 0

    lax.fori_loop(0, 12, step, 0)
    out[...] = (acc[...] * gelu_slope(hidden[...].astype(F32))).astype(BF)


def back_kernel(table, pre, blocks, out, held, sem):
    i = pl.program_id(0)

    @pl.when(i == 0)
    def _():
        load_blocks(blocks, held, sem)

    def step(q, _):
        j = i * 8 + q * 2
        w = blocks_at(held, table, (j, j + 1), list(range(12)), 12)
        part = lax.dot_general(pre[...], w, NT, preferred_element_type=F32).astype(BF)
        for r in range(16):
            out[r % 2, r // 2, :, pl.ds(pl.multiple_of(q * 256, 256), 256)] = part[r * 16 : r * 16 + 16]
        return 0

    lax.fori_loop(0, 4, step, 0)


def grad_kernel(second, feat, hid, live, left, right, out, dense):
    i = pl.program_id(0)
    rows = left.shape[1]
    dense[pl.ds(pl.multiple_of(i * rows, rows), rows)] = lax.dot_general(
        left[...], right[...], TN, preferred_element_type=F32
    ).astype(BF)

    def tile(b):
        got = dense[pl.ds(pl.multiple_of(feat[b] * 32, 32), 32), pl.ds(pl.multiple_of(hid[b] * 128, 128), 128)]
        return jnp.where(b < live[0], got.astype(F32), 0.0)

    @pl.when(i == pl.num_programs(0) - 1)
    def _():
        def four(g, _):
            tiles = [tile(g * 4 + q) for q in range(4)]
            if second:
                turned = jnp.concatenate(tiles, axis=0).T.astype(BF)
                for s in range(8):
                    out[s % 2, s // 2, g] = turned[s * 16 : s * 16 + 16]
            else:
                for q in range(4):
                    got = tiles[q].astype(BF)
                    out[0, g * 4 + q] = got[:16]
                    out[1, g * 4 + q] = got[16:]
            return 0

        lax.fori_loop(0, 72, four, 0)


def scatter_kernel(
    part, one, two, out, first, second, own, mate, total, far_up, far_down, near_up, near_down, last, last_out,
    one_own, one_got, two_own, two_got, two_sum, two_all, send, recv, local,
):
    me = Here()
    greet([me.dev(fc=1), me.dev(fh=1), me.dev(dz=1), me.dev(dz=-1), me.dev(fl=1), me.dev(dx=1), me.dev(dx=-1), me.dev(dx=2)])
    k = Copies(send, recv)
    core, across, side = me.dev(fc=1), me.dev(fh=1), me.dev(fl=1)
    k.send(0, part.at[(me.c + 1) % 2], mate, core)
    k.send(1, two.at[(me.yl + 1) % 2], two_got, side)
    k.send(2, one.at[(me.yl + 1) % 2], one_got, side)
    mine = [
        pltpu.make_async_copy(part.at[me.c], own, local.at[0]),
        pltpu.make_async_copy(two.at[me.yl], two_own, local.at[1]),
        pltpu.make_async_copy(one.at[me.yl], one_own, local.at[2]),
    ]
    for copy in mine:
        copy.start()
    mine[0].wait()
    k.arrived(0, mate, core)

    def add_pair(i, _):
        total[i] = (own[i].astype(F32) + mate[i].astype(F32)).astype(BF)
        return 0

    z2, zu, zd = (me.z + 2) % 4, (me.z + 1) % 4, (me.z + 3) % 4
    lax.fori_loop(z2 * 2, z2 * 2 + 2, add_pair, 0)
    k.send(3, total.at[z2 * 2], far_up, me.dev(dz=1))
    k.send(4, total.at[z2 * 2 + 1], far_down, me.dev(dz=-1))
    lax.fori_loop(zu * 2, zu * 2 + 2, add_pair, 0)
    lax.fori_loop(zd * 2, zd * 2 + 2, add_pair, 0)
    lax.fori_loop(me.z * 2, me.z * 2 + 2, add_pair, 0)
    k.arrived(3, far_up, me.dev(dz=-1))
    total[zu * 2] = (total[zu * 2].astype(F32) + far_up[...].astype(F32)).astype(BF)
    k.send(5, total.at[pl.ds(zu * 2, 2)], near_up, me.dev(dz=1))
    k.arrived(4, far_down, me.dev(dz=1))
    total[zd * 2 + 1] = (total[zd * 2 + 1].astype(F32) + far_down[...].astype(F32)).astype(BF)
    k.send(6, total.at[pl.ds(zd * 2, 2)], near_down, me.dev(dz=-1))

    mine[1].wait()
    k.arrived(1, two_got, side)
    for dx in (2, 1, 3, 0):
        to = (me.x + dx) % 4

        def add_two(g, _):
            two_sum[to, g] = (two_own[to, g].astype(F32) + two_got[to, g].astype(F32)).astype(BF)
            return 0

        lax.fori_loop(0, 72, add_two, 0)
        if dx:
            k.send(6 + dx, two_sum.at[to], two_all.at[me.x], me.dev(dx=dx))
        else:
            two_all[me.x] = two_sum[me.x]

    k.arrived(5, near_up, me.dev(dz=-1))
    k.arrived(6, near_down, me.dev(dz=1))

    def add_three(h):
        return total[me.z * 2 + h].astype(F32) + near_up[h].astype(F32) + near_down[h].astype(F32)

    other = (me.yh + 1) % 2
    last_out[...] = add_three(other).astype(BF)
    k.send(10, last_out, last, across)
    mine[2].wait()
    k.arrived(2, one_got, side)

    def add_one(g, _):
        first[g] = (one_own[g].astype(F32) + one_got[g].astype(F32)).astype(BF)
        return 0

    lax.fori_loop(0, 288, add_one, 0)
    for dx in (1, 2, 3):
        k.arrived(6 + dx, two_all.at[(me.x + 4 - dx) % 4], me.dev(dx=-dx))

    def turn(g, _):
        for q in range(4):
            second[g * 4 + q] = jnp.concatenate([two_all[a, g][:, q * 32 : q * 32 + 32] for a in range(4)], axis=1)
        return 0

    lax.fori_loop(0, 72, turn, 0)
    k.arrived(10, last, across)
    out[...] = (add_three(me.yh) + last[...].astype(F32)).astype(BF)
    k.drain()


def sds(*shape):
    return jax.ShapeDtypeStruct(shape, BF)


def remote(kernel, number, outs, n_in, copies, locals_, scratch=(), specs=None, out_specs=None):
    return pl.pallas_call(
        kernel,
        out_shape=outs,
        in_specs=specs or [ANY] * n_in,
        out_specs=out_specs or tuple([ANY] * len(outs)),
        scratch_shapes=[
            *scratch,
            pltpu.SemaphoreType.DMA((copies,)),
            pltpu.SemaphoreType.DMA((copies,)),
            pltpu.SemaphoreType.DMA((locals_,)),
        ],
        compiler_params=pltpu.CompilerParams(
            collective_id=number, has_side_effects=True, vmem_limit_bytes=56 * MIB
        ),
    )


def shards(inputs, out_grad, hidden_pre, first_blocks, first_feat, first_hid, first_live, second_blocks, second_feat, second_hid, second_live):
    base = lax.axis_index("tensor") * 12
    hid_one, hid_two = first_hid - base, second_hid - base
    slots = jnp.arange(288, dtype=jnp.int32)
    cells = jnp.arange(1152, dtype=jnp.int32)
    cell_one = jnp.where(slots < first_live[0], first_feat * 12 + hid_one, -1)
    cell_two = jnp.where(slots < second_live[0], hid_two * 96 + second_feat, -1)
    table_one = jnp.min(jnp.where(cells[:, None] == cell_one[None], slots[None], 288), axis=1)
    table_two = jnp.min(jnp.where(cells[:, None] == cell_two[None], slots[None], 288), axis=1)
    acts = gelu_value(hidden_pre.astype(F32)).astype(BF)

    def cut(a):
        return a.reshape(16, 96, 4, 32).transpose(2, 0, 1, 3).reshape(4, 16, 3072)

    all_grad, all_acts, in_x, grad_x = remote(
        gather_one, 1, (sds(16, 16, 12288), sds(4, 256, 1536), sds(4, 16, 3072), sds(4, 16, 3072)), 4, 25, 4
    )(out_grad, acts, cut(inputs), cut(out_grad))

    pre = pl.pallas_call(
        pre_kernel,
        out_shape=sds(256, 1536),
        grid=(6,),
        in_specs=[SMEM, VMEM, ANY, pl.BlockSpec((256, 256), lambda k: (0, k))],
        out_specs=pl.BlockSpec((256, 256), lambda k: (0, k)),
        scratch_shapes=[pltpu.VMEM((289, 128, 128), BF), pltpu.VMEM((256, 256), F32), pltpu.SemaphoreType.DMA],
        compiler_params=pltpu.CompilerParams(vmem_limit_bytes=56 * MIB),
    )(table_two, all_grad.reshape(256, 12288), second_blocks, hidden_pre)

    all_pre, in_all, grad_all = remote(
        gather_two, 2, (sds(4, 256, 1536), sds(4, 16, 16, 3072), sds(4, 16, 16, 3072)), 3, 34, 3
    )(pre, in_x, grad_x)

    part = pl.pallas_call(
        back_kernel,
        out_shape=sds(2, 8, 16, 12288),
        grid=(12,),
        in_specs=[SMEM, VMEM, ANY],
        out_specs=pl.BlockSpec((2, 8, 16, 1024), lambda i: (0, 0, 0, i)),
        scratch_shapes=[pltpu.VMEM((289, 128, 128), BF), pltpu.SemaphoreType.DMA],
        compiler_params=pltpu.CompilerParams(vmem_limit_bytes=56 * MIB),
    )(table_one, pre, first_blocks)

    def block_grads(second, feat, hid, live, left, right):
        shape = (2, 4, 72, 16, 128) if second else (2, 288, 16, 128)
        return pl.pallas_call(
            functools.partial(grad_kernel, second),
            out_shape=sds(*shape),
            grid=(6,),
            in_specs=[SMEM, SMEM, SMEM, pl.BlockSpec((1024, 512), lambda i: (0, i)), VMEM],
            out_specs=pl.BlockSpec(shape, lambda i: (0,) * len(shape)),
            scratch_shapes=[pltpu.VMEM((3072, 1536), BF)],
            compiler_params=pltpu.CompilerParams(vmem_limit_bytes=56 * MIB),
        )(feat, hid, live, left.reshape(1024, 3072), right.reshape(1024, 1536))

    two = block_grads(True, second_feat, hid_two, second_live, grad_all, all_acts)
    one = block_grads(False, first_feat, hid_one, first_live, in_all, all_pre)

    pair = (2, 16, 12288)
    return remote(
        scatter_kernel,
        3,
        (sds(16, 12288), sds(288, 16, 128), sds(288, 16, 128)),
        3,
        11,
        3,
        scratch=[
            pltpu.VMEM((8, 16, 12288), BF),
            pltpu.VMEM((8, 16, 12288), BF),
            pltpu.VMEM((8, 16, 12288), BF),
            pltpu.VMEM((16, 12288), BF),
            pltpu.VMEM((16, 12288), BF),
            pltpu.VMEM(pair, BF),
            pltpu.VMEM(pair, BF),
            pltpu.VMEM((16, 12288), BF),
            pltpu.VMEM((16, 12288), BF),
            pltpu.VMEM((288, 16, 128), BF),
            pltpu.VMEM((288, 16, 128), BF),
            pltpu.VMEM((4, 72, 16, 128), BF),
            pltpu.VMEM((4, 72, 16, 128), BF),
            pltpu.VMEM((4, 72, 16, 128), BF),
            pltpu.VMEM((4, 72, 16, 128), BF),
        ],
        out_specs=(VMEM, VMEM, VMEM),
    )(part, one, two)


def solution(mesh):
    rows = P(("seq", "tensor"), None)
    cube = P("tensor", None, None)
    flat = P("tensor")
    in_specs = (rows, rows, P("seq", "tensor"), cube, flat, flat, flat, cube, flat, flat, flat)
    out_specs = (rows, P("tensor", "seq", None), P("tensor", "seq", None))
    return jax.shard_map(shards, mesh=mesh, in_specs=in_specs, out_specs=out_specs, check_vma=False)
```

time: 768 us -> 292 us (0.38)
  waiting for transfers between devices: 453 us -> 0 us
  Pallas kernels: 0 us -> 271 us
  matrix products: 190 us -> 0 us
  local copies, waits for them, and re-layouts: 97.7 us -> 14 us
  between operations: 15.6 us -> 2.03 us
    reduce_scatter x3 -> x0, waiting for transfers between devices: 387 us -> none  [the longest x1 193 us: shards(): lax.psum_scatter(grad_two.astype(jnp.bfloat16), 'seq', scatter_dimension=...]
    pallas_call x0 -> x7, Pallas kernels: none -> 271 us  [the longest x1 65.1 us: shards(): remote(scatter_kernel, 3, (sds(16, 12288), sds(288, 16, 128), sds(288, 16...]
    dot_general x8 -> x0, matrix products: 190 us -> none  [the longest x2 43 us: place_blocks(): jnp.einsum('tbf,bk->tkf', upper, table, preferred_element_type=jnp.float32)]
    all_gather x2 -> x0, waiting for transfers between devices: 64.4 us -> none  [the longest x1 64.4 us: shards(): whole_grad = lax.all_gather(out_grad, 'tensor', axis=0, tiled=True)]
    gather x4 -> x0, local copies, waits for them, and re-layouts: 49.1 us -> none  [the longest x1 14 us: shards(): in_cols = jnp.take(in_tiles, feature_idx, axis=1)]
    all_gather x2 -> x0, local copies, waits for them, and re-layouts: 17.7 us -> none  [the longest x1 9.02 us: shards(): whole_in = lax.all_gather(inputs, 'tensor', axis=0, tiled=True)]
    reshape x4, local copies, waits for them, and re-layouts: 19.5 us -> 8.1 us  [cut(): return a.reshape(16, 96, 4, 32).transpose(2, 0, 1, 3).reshape(4, 16, 3072)]
  transfers between devices with their start and end apart: 5 -> 0, of which waited for: 4 -> 0; matrix products, arithmetic and copies ran while one was open for 39% -> 0% of each run, Pallas kernels for 0% -> 0%
where the time goes in v1:
time: 292 us; the launch traced here: 291 us
  Pallas kernels  271 us (93%)
  local copies, waits for them, and re-layouts  14 us (5%)
  other arithmetic  4.44 us (2%)
    pallas_call x1, Pallas kernels, shards(): remote(scatter_kernel, 3, (sds(16, 12288), sds(288, 16, 128), sds(288, 16...  65.1 us
    pallas_call x1, Pallas kernels, shards(): remote(gather_two, 2, (sds(4, 256, 1536), sds(4, 16, 16, 3072), sds(4, 16...  61.2 us
    pallas_call x1, Pallas kernels, shards(): remote(gather_one, 1, (sds(16, 16, 12288), sds(4, 256, 1536), sds(4, 16,...  47.9 us
    pallas_call x2, Pallas kernels, block_grads(): pl.pallas_call(functools.partial(grad_kernel, second), out_shape=sds(*sha...  38.5 us
    pallas_call x1, Pallas kernels, shards(): pl.pallas_call(pre_kernel, out_shape=sds(256, 1536), grid=(6,), in_specs=...  32.8 us
    pallas_call x1, Pallas kernels, shards(): pl.pallas_call(back_kernel, out_shape=sds(2, 8, 16, 12288), grid=(12,), i...  25.4 us
    reshape x4, local copies, waits for them, and re-layouts, cut(): return a.reshape(16, 96, 4, 32).transpose(2, 0, 1, 3).reshape(4, 16, 3072)  8.1 us

profile of v1, /device:TPU:1, one launch (start us, length us, event | category | flops | bytes accessed | tf_op | source)
XLA Modules:
  0.0 291.4 jit_solution(7043235460685567213)
XLA Ops:
  1.9 1.3 add_select_fusion
  3.2 0.9 select_reduce_fusion.table
  4.1 2.1 reshape.35
  6.2 0.3 copy.18
  6.5 0.0 copy-start.1
  6.5 2.4 reshape.36.in_cut
  8.9 0.0 copy-done.1
  8.9 1.3 reshape.37
  10.1 0.3 copy.19
  10.4 0.0 copy-start
  10.4 2.4 reshape.38.grad_cut
  12.8 1.4 fusion.1.acts
  14.2 47.9 %shard_map.130 = (bf16[16,16,12288]{2,1,0:T(8,128)(2,1)}, bf16[4,256,1536]{2,1,0:T(8,128)(2,1)}, bf16[4,16,3072]{2,1,0:T(8,128)(2,1)}, bf16[4,16,3072]{2,1,0:T(8,128)(2,1)}) custom-call(bf16[16,12288]{1,0:T(8,128)(2,1)} %grad.1, bf16[256,1536]{1,0:T(8,128)(2,1)} %fusion.1.acts, bf16[4,16,3072]{2,1,0:T(8,128)(2,1)} %reshape.36.in_cut, ...), custom_call_target="tpu_custom_call" | custom-call | tf_op jit(solution)/shard_map/pallas_call | solution.py:432
  62.1 32.8 %shard_map.131.pre = bf16[256,1536]{1,0:T(8,128)(2,1)} custom-call(s32[1152]{0:T(1024)} %select_reduce_fusion.table, bf16[256,12288]{1,0:T(8,128)(2,1)} %bitcast.18, bf16[288,128,128]{2,1,0:T(8,128)(2,1)} %blocks.2, bf16[256,1536]{1,0:T(8,128)(2,1)} %hidden.1), custom_call_target="tpu_custom_call" | custom-call | tf_op jit(solution)/shard_map/pallas_call | solution.py:436
  94.9 61.2 %shard_map.133 = (bf16[4,256,1536]{2,1,0:T(8,128)(2,1)}, bf16[4,16,16,3072]{3,2,1,0:T(8,128)(2,1)}, bf16[4,16,16,3072]{3,2,1,0:T(8,128)(2,1)}) custom-call(bf16[256,1536]{1,0:T(8,128)(2,1)} %shard_map.131.pre, bf16[4,16,3072]{2,1,0:T(8,128)(2,1)} %get-tuple-element.11.in_x, bf16[4,16,3072]{2,1,0:T(8,128)(2,1)} %get-tuple-element.12.grad_x), custom_call_target="tpu_custom_call" | custom-call | tf_op jit(solution)/shard_map/pallas_call | solution.py:446
  156.1 16.4 %shard_map.134.one = bf16[2,288,16,128]{3,2,1,0:T(8,128)(2,1)} custom-call(s32[288]{0:T(512)} %feat.2, s32[288]{0:T(512)} %get-tuple-element.22.hid, s32[1]{0:T(128)} %copy.23.live, bf16[1024,3072]{1,0:T(8,128)(2,1)} %bitcast.19, bf16[1024,1536]{1,0:T(8,128)(2,1)} %bitcast.21), custom_call_target="tpu_custom_call" | custom-call | tf_op jit(solution)/shard_map/pallas_call | solution.py:462
  172.4 22.2 %shard_map.135.two = bf16[2,4,72,16,128]{4,3,2,1,0:T(8,128)(2,1)} custom-call(s32[288]{0:T(512)} %feat.3, s32[288]{0:T(512)} %get-tuple-element.18.hid, s32[1]{0:T(128)} %copy.24.live, bf16[1024,3072]{1,0:T(8,128)(2,1)} %bitcast.17, bf16[1024,1536]{1,0:T(8,128)(2,1)} %bitcast.20), custom_call_target="tpu_custom_call" | custom-call | tf_op jit(solution)/shard_map/pallas_call | solution.py:462
  194.6 0.9 select_reduce_fusion.1.table
  195.4 25.4 %shard_map.132.part = bf16[2,8,16,12288]{3,2,1,0:T(8,128)(2,1)} custom-call(s32[1152]{0:T(1024)} %select_reduce_fusion.1.table, bf16[256,1536]{1,0:T(8,128)(2,1)} %shard_map.131.pre, bf16[288,128,128]{2,1,0:T(8,128)(2,1)} %blocks.3), custom_call_target="tpu_custom_call" | custom-call | tf_op jit(solution)/shard_map/pallas_call | solution.py:450
  220.9 65.1 %shard_map.136 = (bf16[16,12288]{1,0:T(8,128)(2,1)}, bf16[288,16,128]{2,1,0:T(8,128)(2,1)}, bf16[288,16,128]{2,1,0:T(8,128)(2,1)}) custom-call(bf16[2,8,16,12288]{3,2,1,0:T(8,128)(2,1)} %shard_map.132.part, bf16[2,288,16,128]{3,2,1,0:T(8,128)(2,1)} %shard_map.134.one, bf16[2,4,72,16,128]{4,3,2,1,0:T(8,128)(2,1)} %shard_map.135.two), custom_call_target="tpu_custom_call" | custom-call | tf_op jit(solution)/shard_map/pallas_call | solution.py:476
  286.0 1.9 copy.25
  287.9 2.5 copy.26
  290.4 0.0 copy-done.2
  290.4 1.0 copy.27
  (2 shorter events, 0.0 us)
Async XLA Ops:
  6.5 2.4 copy-start.1
  10.4 2.4 copy-start
  286.0 4.4 %copy-start.2 = (bf16[288,16,128]{2,1,0:T(8,128)(2,1)S(1)}, bf16[288,16,128]{2,1,0:T(8,128)(2,1)}, u32[]{:S(2)}) copy-start(bf16[288,16,128]{2,1,0:T(8,128)(2,1)} %get-tuple-element.28) | copy-start | bytes 3538948

commit v2 on v1

v2 whole, which is shorter than its diff:
```python
import jax
import jax.numpy as jnp
from jax import lax
from jax.experimental import pallas as pl
from jax.experimental.pallas import tpu as pltpu
from jax.sharding import PartitionSpec as P

MESH = pl.DeviceIdType.MESH
BF = jnp.bfloat16
F32 = jnp.float32
ANY = pl.BlockSpec(memory_space=pl.ANY)
SMEM = pl.BlockSpec(memory_space=pltpu.SMEM)
VMEM = pl.BlockSpec(memory_space=pltpu.VMEM)
MIB = 1024 * 1024

slope_coef = 0.7978845608028654
cubic_coef = 0.044715


def gelu_value(p):
    th = jnp.tanh(slope_coef * (p + cubic_coef * p * p * p))
    return 0.5 * p * (1.0 + th)


def gelu_slope(p):
    th = jnp.tanh(slope_coef * (p + cubic_coef * p * p * p))
    return 0.5 * (1.0 + th) + 0.5 * p * (1.0 - th * th) * slope_coef * (1.0 + 3.0 * cubic_coef * p * p)


class Here:
    def __init__(self):
        s = lax.axis_index("seq")
        t = lax.axis_index("tensor")
        self.s, self.t = s, t
        self.x, self.yl = s // 2, s % 2
        self.z, self.yh, self.c = t // 4, (t // 2) % 2, t % 2

    def dev(self, dx=0, fl=0, dz=0, fh=0, fc=0):
        x = (self.x + dx) % 4
        z = (self.z + dz) % 4
        yl = (self.yl + fl) % 2
        yh = (self.yh + fh) % 2
        c = (self.c + fc) % 2
        return (x * 2 + yl, z * 4 + yh * 2 + c)


class Copies:
    def __init__(self, send, recv):
        self.send_sems, self.recv_sems = send, recv
        self.sent = []

    def send(self, i, src, dst, device):
        copy = pltpu.make_async_remote_copy(
            src_ref=src,
            dst_ref=dst,
            send_sem=self.send_sems.at[i],
            recv_sem=self.recv_sems.at[i],
            device_id=device,
            device_id_type=MESH,
        )
        copy.start()
        self.sent.append(copy)

    def arrived(self, i, dst, device):
        pltpu.make_async_remote_copy(
            src_ref=dst,
            dst_ref=dst,
            send_sem=self.send_sems.at[i],
            recv_sem=self.recv_sems.at[i],
            device_id=device,
            device_id_type=MESH,
        ).wait_recv()

    def drain(self, count=None):
        for copy in self.sent[:count]:
            copy.wait_send()
        self.sent = self.sent[len(self.sent[:count]) :]


def greet(devices):
    barrier = pltpu.get_barrier_semaphore()
    for device in devices:
        pl.semaphore_signal(barrier, inc=1, device_id=device, device_id_type=MESH)
    pl.semaphore_wait(barrier, len(devices))


class TensorGather:
    def __init__(self, me, copies, base, own, slot):
        self.me, self.k, self.b, self.own, self.slot = me, copies, base, own, slot

    def at(self, dz, fh, fc=0):
        me = self.me
        return self.slot(((me.z + dz) % 4) * 4 + ((me.yh + fh) % 2) * 2 + (me.c + fc) % 2)

    def start(self):
        me, k, b, mine = self.me, self.k, self.b, self.at(0, 0)
        k.send(b + 1, self.own, mine, me.dev(fh=1))
        k.send(b + 2, self.own, mine, me.dev(dz=1))
        k.send(b + 3, self.own, mine, me.dev(dz=-1))
        k.send(b + 0, self.own, mine, me.dev(fc=1))

    def spread(self):
        me, k, b = self.me, self.k, self.b
        core = me.dev(fc=1)
        got = self.at(0, 1)
        k.arrived(b + 1, got, me.dev(fh=1))
        k.send(b + 4, got, got, me.dev(dz=1))
        k.send(b + 5, got, got, me.dev(dz=-1))
        k.send(b + 8, got, got, core)
        got = self.at(-1, 0)
        k.arrived(b + 2, got, me.dev(dz=-1))
        k.send(b + 6, got, got, me.dev(dz=1))
        k.send(b + 9, got, got, core)
        got = self.at(1, 0)
        k.arrived(b + 3, got, me.dev(dz=1))
        k.send(b + 11, got, got, core)
        got = self.at(1, 1)
        k.arrived(b + 5, got, me.dev(dz=1))
        k.send(b + 7, got, got, me.dev(dz=-1))
        k.send(b + 12, got, got, core)
        got = self.at(-1, 1)
        k.arrived(b + 4, got, me.dev(dz=-1))
        k.send(b + 10, got, got, core)

    def finish(self):
        me, k, b = self.me, self.k, self.b
        core = me.dev(fc=1)
        got = self.at(2, 0)
        k.arrived(b + 6, got, me.dev(dz=-1))
        k.send(b + 13, got, got, core)
        got = self.at(2, 1)
        k.arrived(b + 7, got, me.dev(dz=1))
        k.send(b + 14, got, got, core)
        for i, dz, fh in ((0, 0, 0), (8, 0, 1), (9, -1, 0), (10, -1, 1), (11, 1, 0), (12, 1, 1), (13, 2, 0), (14, 2, 1)):
            k.arrived(b + i, self.at(dz, fh, 1), core)


class RowGather:
    def __init__(self, me, copies, base, own, slots):
        self.me, self.k, self.b, self.own, self.slots = me, copies, base, own, slots
        self.half = own.shape[0] // 2

    def start(self):
        me, k, b = self.me, self.k, self.b
        k.send(b + 0, self.own, self.slots.at[me.x], me.dev(dx=1))
        k.send(b + 1, self.own, self.slots.at[me.x], me.dev(dx=-1))

    def spread(self):
        me, k, b, half = self.me, self.k, self.b, self.half
        left, right = (me.x + 3) % 4, (me.x + 1) % 4
        k.arrived(b + 0, self.slots.at[left], me.dev(dx=-1))
        part = self.slots.at[left, pl.ds(0, half)]
        k.send(b + 2, part, part, me.dev(dx=1))
        k.arrived(b + 1, self.slots.at[right], me.dev(dx=1))
        part = self.slots.at[right, pl.ds(half, half)]
        k.send(b + 3, part, part, me.dev(dx=-1))

    def finish(self):
        me, k, b, half = self.me, self.k, self.b, self.half
        far = (me.x + 2) % 4
        k.arrived(b + 2, self.slots.at[far, pl.ds(0, half)], me.dev(dx=-1))
        k.arrived(b + 3, self.slots.at[far, pl.ds(half, half)], me.dev(dx=1))


def blocks_at(blocks, table, rows, cols, width):
    return jnp.concatenate(
        [jnp.concatenate([blocks[table[r * width + j]] for j in cols], axis=1) for r in rows], axis=0
    )


NT = (((1,), (1,)), ((), ()))
TN = (((0,), (0,)), ((), ()))


def backward(
    table_one, table_two, tile_one, tile_two, inputs, grad, hidden, blocks_one, blocks_two,
    out, first, second, in_all, grad_all,
    rows, held, all_pre, all_acts, acc, in_cut, grad_cut, in_x, grad_x, mate, far_up, far_down, near_up, near_down, last,
    last_out, dense, lefts, one, one_got, two, two_got, two_sum, two_all, send, recv, local, chunk_sems,
):
    me = Here()
    greet([me.dev(fc=1), me.dev(fh=1), me.dev(dz=1), me.dev(dz=-1), me.dev(fl=1), me.dev(dx=1), me.dev(dx=-1), me.dev(dx=2)])
    k = Copies(send, recv)
    core, across, side = me.dev(fc=1), me.dev(fh=1), me.dev(fl=1)
    whole = TensorGather(me, k, 0, grad, lambda t: rows.at[t])
    grads = TensorGather(me, k, 15, grad_x, lambda t: grad_all.at[:, t])
    ins = TensorGather(me, k, 30, in_x, lambda t: in_all.at[:, t])
    pre_cols = RowGather(me, k, 45, all_pre.at[me.x], all_pre)
    act_cols = RowGather(me, k, 49, all_acts.at[me.x], all_acts)
    whole.start()
    rows[me.t] = grad[...]
    loads = [
        pltpu.make_async_copy(blocks, held.at[pl.ds(0, blocks.shape[0])], local.at[i])
        for i, blocks in enumerate((blocks_two, blocks_one))
    ]
    loads[0].start()
    held[blocks_two.shape[0]] = jnp.zeros(held.shape[1:], held.dtype)
    dense[dense.shape[0] - 1] = jnp.zeros(dense.shape[1:], dense.dtype)

    def cut(source, parts):
        def step(g, _):
            wide = source[:, pl.ds(pl.multiple_of(g * 512, 512), 512)].astype(F32)
            for a in range(4):
                got = jnp.concatenate([wide[:, q * 128 + a * 32 : q * 128 + a * 32 + 32] for q in range(4)], axis=1)
                parts[a, :, pl.ds(pl.multiple_of(g * 128, 128), 128)] = got.astype(BF)
            return 0

        lax.fori_loop(0, 24, step, 0)

    cut(grad, grad_cut)
    for dx in (1, 2, 3):
        k.send(52 + dx, grad_cut.at[(me.x + dx) % 4], grad_x.at[me.x], me.dev(dx=dx))
    cut(inputs, in_cut)
    for dx in (1, 2, 3):
        k.send(55 + dx, in_cut.at[(me.x + dx) % 4], in_x.at[me.x], me.dev(dx=dx))
    grad_x[me.x] = grad_cut[me.x]
    in_x[me.x] = in_cut[me.x]

    def act(i, _):
        span = pl.ds(pl.multiple_of(i * 16, 16), 16)
        all_acts[me.x, span] = gelu_value(hidden[span].astype(F32)).astype(BF)
        return 0

    lax.fori_loop(0, 16, act, 0)
    act_cols.start()
    whole.spread()
    for dx in (1, 2, 3):
        k.arrived(52 + dx, grad_x.at[(me.x + 4 - dx) % 4], me.dev(dx=-dx))
    grads.start()
    mine = [
        pltpu.make_async_copy(grad_x, grad_all.at[:, me.t], local.at[2]),
        pltpu.make_async_copy(in_x, in_all.at[:, me.t], local.at[3]),
    ]
    mine[0].start()
    act_cols.spread()
    for dx in (1, 2, 3):
        k.arrived(55 + dx, in_x.at[(me.x + 4 - dx) % 4], me.dev(dx=-dx))
    mine[1].start()
    whole.finish()
    settled = len(k.sent)
    ins.start()
    loads[0].wait()

    def pre(n, _):
        acc[...] = jnp.zeros_like(acc)

        def step(i, _):
            j = i * 16
            w = blocks_at(held, table_two, (2 * n, 2 * n + 1), [j + a for a in range(16)], 96)
            left = rows[:, :, pl.ds(pl.multiple_of(j * 128, 2048), 2048)].reshape(256, 2048)
            acc[...] += lax.dot_general(left, w, NT, preferred_element_type=F32)
            return 0

        lax.fori_loop(0, 6, step, 0)
        span = pl.ds(pl.multiple_of(n * 256, 256), 256)
        all_pre[me.x, :, span] = (acc[...] * gelu_slope(hidden[:, span].astype(F32))).astype(BF)
        return 0

    lax.fori_loop(0, 2, pre, 0)
    grads.spread()
    lax.fori_loop(2, 4, pre, 0)
    ins.spread()
    lax.fori_loop(4, 6, pre, 0)
    pre_cols.start()
    loads[1].start()

    def block_products(source, right):
        def fetch(i):
            return pltpu.make_async_copy(
                source.at[:, :, :, pl.ds(pl.multiple_of(i * 512, 512), 512)], lefts.at[i % 2], chunk_sems.at[i % 2]
            )

        fetch(0).start()

        def step(i, _):
            @pl.when(i < 5)
            def _():
                fetch(i + 1).start()

            fetch(i).wait()
            got = lax.dot_general(
                lefts[i % 2].reshape(1024, 512), right[...].reshape(1024, 1536), TN, preferred_element_type=F32
            ).astype(BF)
            for a in range(16):
                for h in range(12):
                    dense[(i * 16 + a) * 12 + h] = got[a * 32 : a * 32 + 32, h * 128 : h * 128 + 128]
            return 0

        lax.fori_loop(0, 6, step, 0)

    grads.finish()
    act_cols.finish()
    mine[0].wait()
    block_products(grad_all, all_acts)

    def cut_two(g, _):
        tiles = [dense[tile_two[g * 4 + q]].astype(F32) for q in range(4)]
        turned = jnp.concatenate(tiles, axis=0).T.astype(BF)
        for s in range(8):
            two[s % 2, s // 2, g] = turned[s * 16 : s * 16 + 16]
        return 0

    lax.fori_loop(0, 72, cut_two, 0)
    k.send(65, two.at[(me.yl + 1) % 2], two_got, side)
    pre_cols.spread()
    loads[1].wait()
    k.drain(settled)

    def back(q):
        def step(i, _):
            j = q * 24 + i * 4
            w = blocks_at(held, table_one, [j + a for a in range(4)], list(range(12)), 12)
            got = lax.dot_general(all_pre[me.x], w, NT, preferred_element_type=F32).astype(BF)
            for r in range(16):
                rows[r % 2 * 8 + r // 2, :, pl.ds(pl.multiple_of(j * 128, 512), 512)] = got[r * 16 : r * 16 + 16]
            return 0

        lax.fori_loop(0, 6, step, 0)
        span = pl.ds(q * 3072, 3072)
        k.send(59 + q, rows.at[pl.ds((me.c + 1) % 2 * 8, 8), :, span], mate.at[:, :, span], core)

    back(0)
    back(1)
    ins.finish()
    back(2)
    back(3)
    own = rows.at[pl.ds(me.c * 8, 8)]

    def add_pair(i, _):
        own[i] = (own[i].astype(F32) + mate[i].astype(F32)).astype(BF)
        return 0

    for q in range(4):
        k.arrived(59 + q, mate.at[:, :, pl.ds(q * 3072, 3072)], core)
    z2, zu, zd = (me.z + 2) % 4, (me.z + 1) % 4, (me.z + 3) % 4
    lax.fori_loop(z2 * 2, z2 * 2 + 2, add_pair, 0)
    k.send(63, own.at[z2 * 2], far_up, me.dev(dz=1))
    k.send(64, own.at[z2 * 2 + 1], far_down, me.dev(dz=-1))
    lax.fori_loop(zu * 2, zu * 2 + 2, add_pair, 0)
    lax.fori_loop(zd * 2, zd * 2 + 2, add_pair, 0)
    lax.fori_loop(me.z * 2, me.z * 2 + 2, add_pair, 0)

    k.arrived(63, far_up, me.dev(dz=-1))
    own[zu * 2] = (own[zu * 2].astype(F32) + far_up[...].astype(F32)).astype(BF)
    k.send(66, own.at[pl.ds(zu * 2, 2)], near_up, me.dev(dz=1))
    k.arrived(64, far_down, me.dev(dz=1))
    own[zd * 2 + 1] = (own[zd * 2 + 1].astype(F32) + far_down[...].astype(F32)).astype(BF)
    k.send(67, own.at[pl.ds(zd * 2, 2)], near_down, me.dev(dz=-1))

    pre_cols.finish()
    mine[1].wait()
    block_products(in_all, all_pre)

    def cut_one(g, _):
        for q in range(4):
            b = g * 4 + q
            got = dense[tile_one[b]]
            one[0, b] = got[:16]
            one[1, b] = got[16:]
        return 0

    lax.fori_loop(0, 72, cut_one, 0)
    k.send(68, one.at[(me.yl + 1) % 2], one_got, side)

    k.arrived(66, near_up, me.dev(dz=-1))
    k.arrived(67, near_down, me.dev(dz=1))

    def add_three(h):
        return own[me.z * 2 + h].astype(F32) + near_up[h].astype(F32) + near_down[h].astype(F32)

    last_out[...] = add_three((me.yh + 1) % 2).astype(BF)
    k.send(69, last_out, last, across)

    k.arrived(65, two_got, side)
    for dx in (2, 1, 3, 0):
        to = (me.x + dx) % 4

        def add_two(g, _):
            two_sum[to, g] = (two[me.yl, to, g].astype(F32) + two_got[to, g].astype(F32)).astype(BF)
            return 0

        lax.fori_loop(0, 72, add_two, 0)
        if dx:
            k.send(69 + dx, two_sum.at[to], two_all.at[me.x], me.dev(dx=dx))
        else:
            two_all[me.x] = two_sum[me.x]

    k.arrived(69, last, across)
    out[...] = (add_three(me.yh) + last[...].astype(F32)).astype(BF)
    for dx in (1, 2, 3):
        k.arrived(69 + dx, two_all.at[(me.x + 4 - dx) % 4], me.dev(dx=-dx))

    def turn(g, _):
        for q in range(4):
            second[g * 4 + q] = jnp.concatenate([two_all[a, g][:, q * 32 : q * 32 + 32] for a in range(4)], axis=1)
        return 0

    lax.fori_loop(0, 72, turn, 0)
    k.arrived(68, one_got, side)

    def add_one(g, _):
        first[g] = (one[me.yl, g].astype(F32) + one_got[g].astype(F32)).astype(BF)
        return 0

    lax.fori_loop(0, 288, add_one, 0)
    k.drain()


def sds(*shape):
    return jax.ShapeDtypeStruct(shape, BF)


def shards(inputs, out_grad, hidden_pre, first_blocks, first_feat, first_hid, first_live, second_blocks, second_feat, second_hid, second_live):
    base = lax.axis_index("tensor") * 12
    hid_one, hid_two = first_hid - base, second_hid - base
    slots = jnp.arange(288, dtype=jnp.int32)
    cells = jnp.arange(1152, dtype=jnp.int32)
    cell_one = jnp.where(slots < first_live[0], first_feat * 12 + hid_one, -1)
    cell_two = jnp.where(slots < second_live[0], hid_two * 96 + second_feat, -1)
    table_one = jnp.min(jnp.where(cells[:, None] == cell_one[None], slots[None], 288), axis=1)
    table_two = jnp.min(jnp.where(cells[:, None] == cell_two[None], slots[None], 288), axis=1)
    tile_one = jnp.where(slots < first_live[0], first_feat * 12 + hid_one, 1152)
    tile_two = jnp.where(slots < second_live[0], second_feat * 12 + hid_two, 1152)
    row, pair, half, quarter = (16, 12288), (2, 16, 12288), (8, 16, 12288), (4, 16, 3072)
    shapes = [
        (16, 16, 12288), (289, 128, 128), (4, 256, 1536), (4, 256, 1536), None, quarter, quarter, quarter, quarter, half, row, row,
        pair, pair, row, row, (1153, 32, 128), (2, 4, 16, 16, 512), (2, 288, 16, 128), (288, 16, 128), (2, 4, 72, 16, 128),
        (4, 72, 16, 128), (4, 72, 16, 128), (4, 72, 16, 128),
    ]
    return pl.pallas_call(
        backward,
        out_shape=(sds(*row), sds(288, 16, 128), sds(288, 16, 128), sds(4, 16, 16, 3072), sds(4, 16, 16, 3072)),
        in_specs=[SMEM] * 4 + [VMEM] * 3 + [ANY] * 2,
        out_specs=(VMEM, VMEM, VMEM, ANY, ANY),
        scratch_shapes=[
            *[pltpu.VMEM(shape, BF) if shape else pltpu.VMEM((256, 256), F32) for shape in shapes],
            pltpu.SemaphoreType.DMA((73,)),
            pltpu.SemaphoreType.DMA((73,)),
            pltpu.SemaphoreType.DMA((4,)),
            pltpu.SemaphoreType.DMA((2,)),
        ],
        compiler_params=pltpu.CompilerParams(collective_id=1, has_side_effects=True, vmem_limit_bytes=60 * MIB),
    )(table_one, table_two, tile_one, tile_two, inputs, out_grad, hidden_pre, first_blocks, second_blocks)[:3]


def solution(mesh):
    rows = P(("seq", "tensor"), None)
    cube = P("tensor", None, None)
    flat = P("tensor")
    in_specs = (rows, rows, P("seq", "tensor"), cube, flat, flat, flat, cube, flat, flat, flat)
    out_specs = (rows, P("tensor", "seq", None), P("tensor", "seq", None))
    return jax.shard_map(shards, mesh=mesh, in_specs=in_specs, out_specs=out_specs, check_vma=False)
```

time: 292 us -> 210 us (0.72)
  Pallas kernels: 271 us -> 199 us
  local copies, waits for them, and re-layouts: 14 us -> 5.37 us
    pallas_call x7 -> x1, Pallas kernels: 271 us -> 199 us  [shards(): pl.pallas_call(backward, out_shape=(sds(*row), sds(288, 16, 128), sds(288...]
    reshape x4 -> x0, local copies, waits for them, and re-layouts: 8.1 us -> none  [cut(): return a.reshape(16, 96, 4, 32).transpose(2, 0, 1, 3).reshape(4, 16, 3072)]
where the time goes in v2:
time: 210 us; the launch traced here: 209 us
  Pallas kernels  199 us (95%)
  local copies, waits for them, and re-layouts  5.37 us (3%)
  other arithmetic  3.03 us (1%)
    pallas_call x1, Pallas kernels, shards(): pl.pallas_call(backward, out_shape=(sds(*row), sds(288, 16, 128), sds(288...  199 us
    unnamed x5, local copies, waits for them, and re-layouts  5.37 us

profile of v2, /device:TPU:1, one launch (start us, length us, event | category | flops | bytes accessed | tf_op | source)
XLA Modules:
  0.0 209.2 jit_solution(6290298636036409100)
XLA Ops:
  1.9 1.3 add_select_fusion
  3.2 0.9 select_reduce_fusion.table_two
  4.1 0.9 select_reduce_fusion.1.table_one
  5.0 198.9 %shard_map.130 = (bf16[16,12288]{1,0:T(8,128)(2,1)}, bf16[288,16,128]{2,1,0:T(8,128)(2,1)}, bf16[288,16,128]{2,1,0:T(8,128)(2,1)}, bf16[4,16,16,3072]{3,2,1,0:T(8,128)(2,1)}, bf16[4,16,16,3072]{3,2,1,0:T(8,128)(2,1)}) custom-call(s32[1152]{0:T(1024)} %select_reduce_fusion.1.table_one, s32[1152]{0:T(1024)} %select_reduce_fusion.table_two, ...), custom_call_target="tpu_custom_call" | custom-call | tf_op jit(solution)/shard_map/pallas_call | solution.py:430
  203.8 1.8 copy.19
  205.6 0.0 copy-start
  205.6 2.6 %copy.20 = bf16[288,16,128]{2,1,0:T(8,128)(2,1)} copy(bf16[288,16,128]{2,1,0:T(8,128)(2,1)} %get-tuple-element.19) | data formatting | bytes 2359296
  208.2 0.0 copy-done
  208.2 1.0 copy.21
Async XLA Ops:
  205.6 2.6 %copy-start = (bf16[288,16,128]{2,1,0:T(8,128)(2,1)S(1)}, bf16[288,16,128]{2,1,0:T(8,128)(2,1)}, u32[]{:S(2)}) copy-start(bf16[288,16,128]{2,1,0:T(8,128)(2,1)} %get-tuple-element.20) | copy-start | bytes 3538948

commit v3 on v2

--- a/solution.py
+++ b/solution.py
@@ -162,6 +162,52 @@
         k.arrived(b + 3, self.slots.at[far, pl.ds(half, half)], me.dev(dx=1))
 
 
+class SeqGather:
+    def __init__(self, me, copies, base, slots):
+        self.me, self.k, self.b, self.slots = me, copies, base, slots
+
+    def at(self, dx, fl):
+        me = self.me
+        return self.slots.at[(me.x + dx) % 4 * 2 + (me.yl + fl) % 2]
+
+    def half(self, dx, i):
+        me = self.me
+        return self.slots.at[(me.x + dx) % 4 * 2 + me.yl, pl.ds(i * 128, 128)]
+
+    def start(self):
+        me, k, b = self.me, self.k, self.b
+        own = self.at(0, 0)
+        k.send(b + 2, own, own, me.dev(fl=1))
+        k.send(b + 0, own, own, me.dev(dx=1))
+        k.send(b + 1, own, own, me.dev(dx=-1))
+
+    def spread(self):
+        me, k, b = self.me, self.k, self.b
+        k.arrived(b + 0, self.at(-1, 0), me.dev(dx=-1))
+        part = self.half(-1, 0)
+        k.send(b + 3, part, part, me.dev(dx=1))
+        k.arrived(b + 1, self.at(1, 0), me.dev(dx=1))
+        part = self.half(1, 1)
+        k.send(b + 4, part, part, me.dev(dx=-1))
+        got = self.at(0, 1)
+        k.arrived(b + 2, got, me.dev(fl=1))
+        k.send(b + 5, got, got, me.dev(dx=1))
+        k.send(b + 6, got, got, me.dev(dx=-1))
+
+    def cross(self):
+        me, k, b = self.me, self.k, self.b
+        k.arrived(b + 3, self.half(2, 0), me.dev(dx=-1))
+        k.arrived(b + 4, self.half(2, 1), me.dev(dx=1))
+        got = self.at(2, 0)
+        k.send(b + 7, got, got, me.dev(fl=1))
+
+    def finish(self):
+        me, k, b = self.me, self.k, self.b
+        k.arrived(b + 5, self.at(-1, 1), me.dev(dx=-1))
+        k.arrived(b + 6, self.at(1, 1), me.dev(dx=1))
+        k.arrived(b + 7, self.at(2, 1), me.dev(fl=1))
+
+
 def blocks_at(blocks, table, rows, cols, width):
     return jnp.concatenate(
         [jnp.concatenate([blocks[table[r * width + j]] for j in cols], axis=1) for r in rows], axis=0
@@ -176,17 +222,17 @@
     table_one, table_two, tile_one, tile_two, inputs, grad, hidden, blocks_one, blocks_two,
     out, first, second, in_all, grad_all,
     rows, held, all_pre, all_acts, acc, in_cut, grad_cut, in_x, grad_x, mate, far_up, far_down, near_up, near_down, last,
-    last_out, dense, lefts, one, one_got, two, two_got, two_sum, two_all, send, recv, local, chunk_sems,
+    last_out, dense, lefts, in_lefts, two, two_got, two_sum, two_all, send, recv, local, chunk_sems,
 ):
     me = Here()
-    greet([me.dev(fc=1), me.dev(fh=1), me.dev(dz=1), me.dev(dz=-1), me.dev(fl=1), me.dev(dx=1), me.dev(dx=-1), me.dev(dx=2)])
+    greet([me.dev(fc=1), me.dev(fh=1), me.dev(dz=1), me.dev(dz=-1), me.dev(fl=1), me.dev(dx=1), me.dev(dx=-1), me.dev(dx=2)] + [me.dev(dx=dx, fl=1) for dx in (1, 2, 3)])
     k = Copies(send, recv)
     core, across, side = me.dev(fc=1), me.dev(fh=1), me.dev(fl=1)
     whole = TensorGather(me, k, 0, grad, lambda t: rows.at[t])
     grads = TensorGather(me, k, 15, grad_x, lambda t: grad_all.at[:, t])
     ins = TensorGather(me, k, 30, in_x, lambda t: in_all.at[:, t])
-    pre_cols = RowGather(me, k, 45, all_pre.at[me.x], all_pre)
-    act_cols = RowGather(me, k, 49, all_acts.at[me.x], all_acts)
+    pre_cols = SeqGather(me, k, 45, all_pre)
+    act_cols = RowGather(me, k, 53, all_acts.at[me.x], all_acts)
     whole.start()
     rows[me.t] = grad[...]
     loads = [
@@ -197,24 +243,22 @@
     held[blocks_two.shape[0]] = jnp.zeros(held.shape[1:], held.dtype)
     dense[dense.shape[0] - 1] = jnp.zeros(dense.shape[1:], dense.dtype)
 
-    def cut(source, parts):
+    def cut(source, parts, n):
+        wide, thin = n * 128, 128 // n
+
         def step(g, _):
-            wide = source[:, pl.ds(pl.multiple_of(g * 512, 512), 512)].astype(F32)
-            for a in range(4):
-                got = jnp.concatenate([wide[:, q * 128 + a * 32 : q * 128 + a * 32 + 32] for q in range(4)], axis=1)
-                parts[a, :, pl.ds(pl.multiple_of(g * 128, 128), 128)] = got.astype(BF)
+            got = source[:, pl.ds(pl.multiple_of(g * wide, wide), wide)].astype(F32)
+            for a in range(n):
+                part = jnp.concatenate([got[:, q * 128 + a * thin : q * 128 + a * thin + thin] for q in range(n)], axis=1)
+                parts[a, :, pl.ds(pl.multiple_of(g * 128, 128), 128)] = part.astype(BF)
             return 0
 
-        lax.fori_loop(0, 24, step, 0)
-
-    cut(grad, grad_cut)
+        lax.fori_loop(0, 96 // n, step, 0)
+
+    cut(grad, grad_cut, 4)
     for dx in (1, 2, 3):
-        k.send(52 + dx, grad_cut.at[(me.x + dx) % 4], grad_x.at[me.x], me.dev(dx=dx))
-    cut(inputs, in_cut)
-    for dx in (1, 2, 3):
-        k.send(55 + dx, in_cut.at[(me.x + dx) % 4], in_x.at[me.x], me.dev(dx=dx))
+        k.send(56 + dx, grad_cut.at[(me.x + dx) % 4], grad_x.at[me.x], me.dev(dx=dx))
     grad_x[me.x] = grad_cut[me.x]
-    in_x[me.x] = in_cut[me.x]
 
     def act(i, _):
         span = pl.ds(pl.multiple_of(i * 16, 16), 16)
@@ -225,20 +269,22 @@
     act_cols.start()
     whole.spread()
     for dx in (1, 2, 3):
-        k.arrived(52 + dx, grad_x.at[(me.x + 4 - dx) % 4], me.dev(dx=-dx))
+        k.arrived(56 + dx, grad_x.at[(me.x + 4 - dx) % 4], me.dev(dx=-dx))
     grads.start()
     mine = [
         pltpu.make_async_copy(grad_x, grad_all.at[:, me.t], local.at[2]),
         pltpu.make_async_copy(in_x, in_all.at[:, me.t], local.at[3]),
     ]
     mine[0].start()
+    cut(inputs, in_cut, 8)
+    others = [(dx, fl) for dx in range(4) for fl in range(2)][1:]
+    for i, (dx, fl) in enumerate(others):
+        to = (me.x + dx) % 4 * 2 + (me.yl + fl) % 2
+        k.send(60 + i, in_cut.at[to], in_x.at[me.s], me.dev(dx=dx, fl=fl))
+    in_x[me.s] = in_cut[me.s]
     act_cols.spread()
-    for dx in (1, 2, 3):
-        k.arrived(55 + dx, in_x.at[(me.x + 4 - dx) % 4], me.dev(dx=-dx))
-    mine[1].start()
     whole.finish()
     settled = len(k.sent)
-    ins.start()
     loads[0].wait()
 
     def pre(n, _):
@@ -253,24 +299,31 @@
 
         lax.fori_loop(0, 6, step, 0)
         span = pl.ds(pl.multiple_of(n * 256, 256), 256)
-        all_pre[me.x, :, span] = (acc[...] * gelu_slope(hidden[:, span].astype(F32))).astype(BF)
+        all_pre[me.s, :, span] = (acc[...] * gelu_slope(hidden[:, span].astype(F32))).astype(BF)
         return 0
 
     lax.fori_loop(0, 2, pre, 0)
     grads.spread()
     lax.fori_loop(2, 4, pre, 0)
-    ins.spread()
+    for i, (dx, fl) in enumerate(others):
+        k.arrived(60 + i, in_x.at[(me.x + 4 - dx) % 4 * 2 + (me.yl + fl) % 2], me.dev(dx=-dx, fl=fl))
+    mine[1].start()
+    ins.start()
     lax.fori_loop(4, 6, pre, 0)
     pre_cols.start()
     loads[1].start()
 
-    def block_products(source, right):
+    def block_products(source, buffers, right, cuts, first_step, last_step):
+        tall, wide = cuts * 256, 2048 // cuts
+        thin = wide // 16
+
         def fetch(i):
             return pltpu.make_async_copy(
-                source.at[:, :, :, pl.ds(pl.multiple_of(i * 512, 512), 512)], lefts.at[i % 2], chunk_sems.at[i % 2]
+                source.at[:, :, :, pl.ds(pl.multiple_of(i * wide, wide), wide)], buffers.at[i % 2], chunk_sems.at[i % 2]
             )
 
-        fetch(0).start()
+        if first_step == 0:
+            fetch(0).start()
 
         def step(i, _):
             @pl.when(i < 5)
@@ -279,19 +332,21 @@
 
             fetch(i).wait()
             got = lax.dot_general(
-                lefts[i % 2].reshape(1024, 512), right[...].reshape(1024, 1536), TN, preferred_element_type=F32
+                buffers[i % 2].reshape(tall, wide), right[...].reshape(tall, 1536), TN, preferred_element_type=F32
             ).astype(BF)
             for a in range(16):
                 for h in range(12):
-                    dense[(i * 16 + a) * 12 + h] = got[a * 32 : a * 32 + 32, h * 128 : h * 128 + 128]
+                    dense[(i * 16 + a) * 12 + h, :thin] = got[a * thin : a * thin + thin, h * 128 : h * 128 + 128]
             return 0
 
-        lax.fori_loop(0, 6, step, 0)
+        lax.fori_loop(first_step, last_step, step, 0)
 
     grads.finish()
     act_cols.finish()
     mine[0].wait()
-    block_products(grad_all, all_acts)
+    block_products(grad_all, lefts, all_acts, 4, 0, 6)
+    ins.spread()
+    pre_cols.spread()
 
     def cut_two(g, _):
         tiles = [dense[tile_two[g * 4 + q]].astype(F32) for q in range(4)]
@@ -301,8 +356,7 @@
         return 0
 
     lax.fori_loop(0, 72, cut_two, 0)
-    k.send(65, two.at[(me.yl + 1) % 2], two_got, side)
-    pre_cols.spread()
+    k.send(73, two.at[(me.yl + 1) % 2], two_got, side)
     loads[1].wait()
     k.drain(settled)
 
@@ -310,20 +364,21 @@
         def step(i, _):
             j = q * 24 + i * 4
             w = blocks_at(held, table_one, [j + a for a in range(4)], list(range(12)), 12)
-            got = lax.dot_general(all_pre[me.x], w, NT, preferred_element_type=F32).astype(BF)
+            got = lax.dot_general(all_pre[me.s], w, NT, preferred_element_type=F32).astype(BF)
             for r in range(16):
                 rows[r % 2 * 8 + r // 2, :, pl.ds(pl.multiple_of(j * 128, 512), 512)] = got[r * 16 : r * 16 + 16]
             return 0
 
         lax.fori_loop(0, 6, step, 0)
         span = pl.ds(q * 3072, 3072)
-        k.send(59 + q, rows.at[pl.ds((me.c + 1) % 2 * 8, 8), :, span], mate.at[:, :, span], core)
+        k.send(67 + q, rows.at[pl.ds((me.c + 1) % 2 * 8, 8), :, span], mate.at[:, :, span], core)
 
     back(0)
     back(1)
+    back(2)
+    pre_cols.cross()
+    back(3)
     ins.finish()
-    back(2)
-    back(3)
     own = rows.at[pl.ds(me.c * 8, 8)]
 
     def add_pair(i, _):
@@ -331,47 +386,27 @@
         return 0
 
     for q in range(4):
-        k.arrived(59 + q, mate.at[:, :, pl.ds(q * 3072, 3072)], core)
+        k.arrived(67 + q, mate.at[:, :, pl.ds(q * 3072, 3072)], core)
     z2, zu, zd = (me.z + 2) % 4, (me.z + 1) % 4, (me.z + 3) % 4
     lax.fori_loop(z2 * 2, z2 * 2 + 2, add_pair, 0)
-    k.send(63, own.at[z2 * 2], far_up, me.dev(dz=1))
-    k.send(64, own.at[z2 * 2 + 1], far_down, me.dev(dz=-1))
+    k.send(71, own.at[z2 * 2], far_up, me.dev(dz=1))
+    k.send(72, own.at[z2 * 2 + 1], far_down, me.dev(dz=-1))
     lax.fori_loop(zu * 2, zu * 2 + 2, add_pair, 0)
     lax.fori_loop(zd * 2, zd * 2 + 2, add_pair, 0)
     lax.fori_loop(me.z * 2, me.z * 2 + 2, add_pair, 0)
 
-    k.arrived(63, far_up, me.dev(dz=-1))
-    own[zu * 2] = (own[zu * 2].astype(F32) + far_up[...].astype(F32)).astype(BF)
-    k.send(66, own.at[pl.ds(zu * 2, 2)], near_up, me.dev(dz=1))
-    k.arrived(64, far_down, me.dev(dz=1))
-    own[zd * 2 + 1] = (own[zd * 2 + 1].astype(F32) + far_down[...].astype(F32)).astype(BF)
-    k.send(67, own.at[pl.ds(zd * 2, 2)], near_down, me.dev(dz=-1))
-
     pre_cols.finish()
     mine[1].wait()
-    block_products(in_all, all_pre)
-
-    def cut_one(g, _):
-        for q in range(4):
-            b = g * 4 + q
-            got = dense[tile_one[b]]
-            one[0, b] = got[:16]
-            one[1, b] = got[16:]
-        return 0
-
-    lax.fori_loop(0, 72, cut_one, 0)
-    k.send(68, one.at[(me.yl + 1) % 2], one_got, side)
-
-    k.arrived(66, near_up, me.dev(dz=-1))
-    k.arrived(67, near_down, me.dev(dz=1))
-
-    def add_three(h):
-        return own[me.z * 2 + h].astype(F32) + near_up[h].astype(F32) + near_down[h].astype(F32)
-
-    last_out[...] = add_three((me.yh + 1) % 2).astype(BF)
-    k.send(69, last_out, last, across)
-
-    k.arrived(65, two_got, side)
+    block_products(in_all, in_lefts, all_pre, 8, 0, 3)
+
+    k.arrived(71, far_up, me.dev(dz=-1))
+    own[zu * 2] = (own[zu * 2].astype(F32) + far_up[...].astype(F32)).astype(BF)
+    k.send(74, own.at[pl.ds(zu * 2, 2)], near_up, me.dev(dz=1))
+    k.arrived(72, far_down, me.dev(dz=1))
+    own[zd * 2 + 1] = (own[zd * 2 + 1].astype(F32) + far_down[...].astype(F32)).astype(BF)
+    k.send(75, own.at[pl.ds(zd * 2, 2)], near_down, me.dev(dz=-1))
+
+    k.arrived(73, two_got, side)
     for dx in (2, 1, 3, 0):
         to = (me.x + dx) % 4
 
@@ -381,14 +416,29 @@
 
         lax.fori_loop(0, 72, add_two, 0)
         if dx:
-            k.send(69 + dx, two_sum.at[to], two_all.at[me.x], me.dev(dx=dx))
+            k.send(76 + dx, two_sum.at[to], two_all.at[me.x], me.dev(dx=dx))
         else:
             two_all[me.x] = two_sum[me.x]
 
-    k.arrived(69, last, across)
-    out[...] = (add_three(me.yh) + last[...].astype(F32)).astype(BF)
+    block_products(in_all, in_lefts, all_pre, 8, 3, 6)
+
+    k.arrived(74, near_up, me.dev(dz=-1))
+    k.arrived(75, near_down, me.dev(dz=1))
+
+    def add_three(h):
+        return own[me.z * 2 + h].astype(F32) + near_up[h].astype(F32) + near_down[h].astype(F32)
+
+    last_out[...] = add_three((me.yh + 1) % 2).astype(BF)
+    k.send(76, last_out, last, across)
+
+    def cut_one(g, _):
+        for q in range(4):
+            first[g * 4 + q] = dense[tile_one[g * 4 + q]][:16]
+        return 0
+
+    lax.fori_loop(0, 72, cut_one, 0)
     for dx in (1, 2, 3):
-        k.arrived(69 + dx, two_all.at[(me.x + 4 - dx) % 4], me.dev(dx=-dx))
+        k.arrived(76 + dx, two_all.at[(me.x + 4 - dx) % 4], me.dev(dx=-dx))
 
     def turn(g, _):
         for q in range(4):
@@ -396,13 +446,8 @@
         return 0
 
     lax.fori_loop(0, 72, turn, 0)
-    k.arrived(68, one_got, side)
-
-    def add_one(g, _):
-        first[g] = (one[me.yl, g].astype(F32) + one_got[g].astype(F32)).astype(BF)
-        return 0
-
-    lax.fori_loop(0, 288, add_one, 0)
+    k.arrived(76, last, across)
+    out[...] = (add_three(me.yh) + last[...].astype(F32)).astype(BF)
     k.drain()
 
 
@@ -421,21 +466,21 @@
     table_two = jnp.min(jnp.where(cells[:, None] == cell_two[None], slots[None], 288), axis=1)
     tile_one = jnp.where(slots < first_live[0], first_feat * 12 + hid_one, 1152)
     tile_two = jnp.where(slots < second_live[0], second_feat * 12 + hid_two, 1152)
-    row, pair, half, quarter = (16, 12288), (2, 16, 12288), (8, 16, 12288), (4, 16, 3072)
+    row, pair, half, quarter, eighth = (16, 12288), (2, 16, 12288), (8, 16, 12288), (4, 16, 3072), (8, 16, 1536)
     shapes = [
-        (16, 16, 12288), (289, 128, 128), (4, 256, 1536), (4, 256, 1536), None, quarter, quarter, quarter, quarter, half, row, row,
-        pair, pair, row, row, (1153, 32, 128), (2, 4, 16, 16, 512), (2, 288, 16, 128), (288, 16, 128), (2, 4, 72, 16, 128),
+        (16, 16, 12288), (289, 128, 128), (8, 256, 1536), (4, 256, 1536), None, eighth, quarter, eighth, quarter, half, row, row,
+        pair, pair, row, row, (1153, 32, 128), (2, 4, 16, 16, 512), (2, 8, 16, 16, 256), (2, 4, 72, 16, 128),
         (4, 72, 16, 128), (4, 72, 16, 128), (4, 72, 16, 128),
     ]
     return pl.pallas_call(
         backward,
-        out_shape=(sds(*row), sds(288, 16, 128), sds(288, 16, 128), sds(4, 16, 16, 3072), sds(4, 16, 16, 3072)),
+        out_shape=(sds(*row), sds(288, 16, 128), sds(288, 16, 128), sds(8, 16, 16, 1536), sds(4, 16, 16, 3072)),
         in_specs=[SMEM] * 4 + [VMEM] * 3 + [ANY] * 2,
         out_specs=(VMEM, VMEM, VMEM, ANY, ANY),
         scratch_shapes=[
             *[pltpu.VMEM(shape, BF) if shape else pltpu.VMEM((256, 256), F32) for shape in shapes],
-            pltpu.SemaphoreType.DMA((73,)),
-            pltpu.SemaphoreType.DMA((73,)),
+            pltpu.SemaphoreType.DMA((80,)),
+            pltpu.SemaphoreType.DMA((80,)),
             pltpu.SemaphoreType.DMA((4,)),
             pltpu.SemaphoreType.DMA((2,)),
         ],

time: 210 us -> 198 us (0.943)
  Pallas kernels: 199 us -> 186 us
    pallas_call x1, Pallas kernels: 199 us -> 186 us  [shards(): pl.pallas_call(backward, out_shape=(sds(*row), sds(288, 16, 128), sds(288...]
where the time goes in v3:
time: 198 us; the launch traced here: 196 us
  Pallas kernels  186 us (94%)
  local copies, waits for them, and re-layouts  5.37 us (3%)
  other arithmetic  3.03 us (2%)
    pallas_call x1, Pallas kernels, shards(): pl.pallas_call(backward, out_shape=(sds(*row), sds(288, 16, 128), sds(288...  186 us
    unnamed x5, local copies, waits for them, and re-layouts  5.37 us

profile of v3, /device:TPU:1, one launch (start us, length us, event | category | flops | bytes accessed | tf_op | source)
XLA Modules:
  0.0 195.9 jit_solution(16053424226310765650)
XLA Ops:
  1.9 1.3 add_select_fusion
  3.2 0.9 select_reduce_fusion.table_two
  4.1 0.9 select_reduce_fusion.1.table_one
  5.0 185.5 %shard_map.130 = (bf16[16,12288]{1,0:T(8,128)(2,1)}, bf16[288,16,128]{2,1,0:T(8,128)(2,1)}, bf16[288,16,128]{2,1,0:T(8,128)(2,1)}, bf16[8,16,16,1536]{3,2,1,0:T(8,128)(2,1)}, bf16[4,16,16,3072]{3,2,1,0:T(8,128)(2,1)}) custom-call(s32[1152]{0:T(1024)} %select_reduce_fusion.1.table_one, s32[1152]{0:T(1024)} %select_reduce_fusion.table_two, ...), custom_call_target="tpu_custom_call" | custom-call | tf_op jit(solution)/shard_map/pallas_call | solution.py:475
  190.5 1.8 copy.19
  192.3 0.0 copy-start
  192.3 2.6 %copy.20 = bf16[288,16,128]{2,1,0:T(8,128)(2,1)} copy(bf16[288,16,128]{2,1,0:T(8,128)(2,1)} %get-tuple-element.19) | data formatting | bytes 2359296
  194.8 0.0 copy-done
  194.8 1.0 copy.21
Async XLA Ops:
  192.3 2.6 %copy-start = (bf16[288,16,128]{2,1,0:T(8,128)(2,1)S(1)}, bf16[288,16,128]{2,1,0:T(8,128)(2,1)}, u32[]{:S(2)}) copy-start(bf16[288,16,128]{2,1,0:T(8,128)(2,1)} %get-tuple-element.20) | copy-start | bytes 3538948

commit v4 on v3

--- a/solution.py
+++ b/solution.py
@@ -114,6 +114,10 @@
         got = self.at(1, 0)
         k.arrived(b + 3, got, me.dev(dz=1))
         k.send(b + 11, got, got, core)
+
+    def middle(self):
+        me, k, b = self.me, self.k, self.b
+        core = me.dev(fc=1)
         got = self.at(1, 1)
         k.arrived(b + 5, got, me.dev(dz=1))
         k.send(b + 7, got, got, me.dev(dz=-1))
@@ -170,9 +174,9 @@
         me = self.me
         return self.slots.at[(me.x + dx) % 4 * 2 + (me.yl + fl) % 2]
 
-    def half(self, dx, i):
+    def half(self, dx, fl, i):
         me = self.me
-        return self.slots.at[(me.x + dx) % 4 * 2 + me.yl, pl.ds(i * 128, 128)]
+        return self.slots.at[(me.x + dx) % 4 * 2 + (me.yl + fl) % 2, pl.ds(i * 128, 128)]
 
     def start(self):
         me, k, b = self.me, self.k, self.b
@@ -184,10 +188,10 @@
     def spread(self):
         me, k, b = self.me, self.k, self.b
         k.arrived(b + 0, self.at(-1, 0), me.dev(dx=-1))
-        part = self.half(-1, 0)
+        part = self.half(-1, 0, 0)
         k.send(b + 3, part, part, me.dev(dx=1))
         k.arrived(b + 1, self.at(1, 0), me.dev(dx=1))
-        part = self.half(1, 1)
+        part = self.half(1, 0, 1)
         k.send(b + 4, part, part, me.dev(dx=-1))
         got = self.at(0, 1)
         k.arrived(b + 2, got, me.dev(fl=1))
@@ -196,16 +200,18 @@
 
     def cross(self):
         me, k, b = self.me, self.k, self.b
-        k.arrived(b + 3, self.half(2, 0), me.dev(dx=-1))
-        k.arrived(b + 4, self.half(2, 1), me.dev(dx=1))
-        got = self.at(2, 0)
-        k.send(b + 7, got, got, me.dev(fl=1))
+        k.arrived(b + 5, self.at(-1, 1), me.dev(dx=-1))
+        part = self.half(-1, 1, 0)
+        k.send(b + 7, part, part, me.dev(dx=1))
+        k.arrived(b + 6, self.at(1, 1), me.dev(dx=1))
+        part = self.half(1, 1, 1)
+        k.send(b + 8, part, part, me.dev(dx=-1))
 
     def finish(self):
         me, k, b = self.me, self.k, self.b
-        k.arrived(b + 5, self.at(-1, 1), me.dev(dx=-1))
-        k.arrived(b + 6, self.at(1, 1), me.dev(dx=1))
-        k.arrived(b + 7, self.at(2, 1), me.dev(fl=1))
+        for i, fl in ((3, 0), (7, 1)):
+            k.arrived(b + i, self.half(2, fl, 0), me.dev(dx=-1))
+            k.arrived(b + i + 1, self.half(2, fl, 1), me.dev(dx=1))
 
 
 def blocks_at(blocks, table, rows, cols, width):
@@ -232,7 +238,7 @@
     grads = TensorGather(me, k, 15, grad_x, lambda t: grad_all.at[:, t])
     ins = TensorGather(me, k, 30, in_x, lambda t: in_all.at[:, t])
     pre_cols = SeqGather(me, k, 45, all_pre)
-    act_cols = RowGather(me, k, 53, all_acts.at[me.x], all_acts)
+    act_cols = RowGather(me, k, 80, all_acts.at[me.x], all_acts)
     whole.start()
     rows[me.t] = grad[...]
     loads = [
@@ -268,6 +274,13 @@
     lax.fori_loop(0, 16, act, 0)
     act_cols.start()
     whole.spread()
+    cut(inputs, in_cut, 8)
+    others = [(dx, fl) for dx in range(4) for fl in range(2)][1:]
+    for i, (dx, fl) in enumerate(others):
+        to = (me.x + dx) % 4 * 2 + (me.yl + fl) % 2
+        k.send(60 + i, in_cut.at[to], in_x.at[me.s], me.dev(dx=dx, fl=fl))
+    in_x[me.s] = in_cut[me.s]
+    whole.middle()
     for dx in (1, 2, 3):
         k.arrived(56 + dx, grad_x.at[(me.x + 4 - dx) % 4], me.dev(dx=-dx))
     grads.start()
@@ -276,12 +289,6 @@
         pltpu.make_async_copy(in_x, in_all.at[:, me.t], local.at[3]),
     ]
     mine[0].start()
-    cut(inputs, in_cut, 8)
-    others = [(dx, fl) for dx in range(4) for fl in range(2)][1:]
-    for i, (dx, fl) in enumerate(others):
-        to = (me.x + dx) % 4 * 2 + (me.yl + fl) % 2
-        k.send(60 + i, in_cut.at[to], in_x.at[me.s], me.dev(dx=dx, fl=fl))
-    in_x[me.s] = in_cut[me.s]
     act_cols.spread()
     whole.finish()
     settled = len(k.sent)
@@ -308,6 +315,7 @@
     for i, (dx, fl) in enumerate(others):
         k.arrived(60 + i, in_x.at[(me.x + 4 - dx) % 4 * 2 + (me.yl + fl) % 2], me.dev(dx=-dx, fl=fl))
     mine[1].start()
+    grads.middle()
     ins.start()
     lax.fori_loop(4, 6, pre, 0)
     pre_cols.start()
@@ -344,9 +352,9 @@
     grads.finish()
     act_cols.finish()
     mine[0].wait()
-    block_products(grad_all, lefts, all_acts, 4, 0, 6)
+    block_products(grad_all, lefts, all_acts, 4, 0, 3)
     ins.spread()
-    pre_cols.spread()
+    block_products(grad_all, lefts, all_acts, 4, 3, 6)
 
     def cut_two(g, _):
         tiles = [dense[tile_two[g * 4 + q]].astype(F32) for q in range(4)]
@@ -357,6 +365,8 @@
 
     lax.fori_loop(0, 72, cut_two, 0)
     k.send(73, two.at[(me.yl + 1) % 2], two_got, side)
+    pre_cols.spread()
+    ins.middle()
     loads[1].wait()
     k.drain(settled)
 
@@ -376,9 +386,7 @@
     back(0)
     back(1)
     back(2)
-    pre_cols.cross()
     back(3)
-    ins.finish()
     own = rows.at[pl.ds(me.c * 8, 8)]
 
     def add_pair(i, _):
@@ -395,16 +403,18 @@
     lax.fori_loop(zd * 2, zd * 2 + 2, add_pair, 0)
     lax.fori_loop(me.z * 2, me.z * 2 + 2, add_pair, 0)
 
-    pre_cols.finish()
-    mine[1].wait()
-    block_products(in_all, in_lefts, all_pre, 8, 0, 3)
-
+    ins.finish()
+    pre_cols.cross()
     k.arrived(71, far_up, me.dev(dz=-1))
     own[zu * 2] = (own[zu * 2].astype(F32) + far_up[...].astype(F32)).astype(BF)
     k.send(74, own.at[pl.ds(zu * 2, 2)], near_up, me.dev(dz=1))
     k.arrived(72, far_down, me.dev(dz=1))
     own[zd * 2 + 1] = (own[zd * 2 + 1].astype(F32) + far_down[...].astype(F32)).astype(BF)
     k.send(75, own.at[pl.ds(zd * 2, 2)], near_down, me.dev(dz=-1))
+
+    pre_cols.finish()
+    mine[1].wait()
+    block_products(in_all, in_lefts, all_pre, 8, 0, 3)
 
     k.arrived(73, two_got, side)
     for dx in (2, 1, 3, 0):
@@ -479,8 +489,8 @@
         out_specs=(VMEM, VMEM, VMEM, ANY, ANY),
         scratch_shapes=[
             *[pltpu.VMEM(shape, BF) if shape else pltpu.VMEM((256, 256), F32) for shape in shapes],
-            pltpu.SemaphoreType.DMA((80,)),
-            pltpu.SemaphoreType.DMA((80,)),
+            pltpu.SemaphoreType.DMA((84,)),
+            pltpu.SemaphoreType.DMA((84,)),
             pltpu.SemaphoreType.DMA((4,)),
             pltpu.SemaphoreType.DMA((2,)),
         ],

time: 198 us -> 167 us (0.84)
  Pallas kernels: 186 us -> 156 us
    pallas_call x1, Pallas kernels: 186 us -> 156 us  [shards(): pl.pallas_call(backward, out_shape=(sds(*row), sds(288, 16, 128), sds(288...]
where the time goes in v4:
time: 167 us; the launch traced here: 166 us
  Pallas kernels  156 us (93%)
  local copies, waits for them, and re-layouts  5.37 us (3%)
  other arithmetic  3.03 us (2%)
  between operations  1.94 us (1%)
    pallas_call x1, Pallas kernels, shards(): pl.pallas_call(backward, out_shape=(sds(*row), sds(288, 16, 128), sds(288...  156 us
    unnamed x5, local copies, waits for them, and re-layouts  5.37 us

profile of v4, /device:TPU:1, one launch (start us, length us, event | category | flops | bytes accessed | tf_op | source)
XLA Modules:
  0.0 166.2 jit_solution(1744275889516418566)
XLA Ops:
  1.9 1.3 add_select_fusion
  3.2 0.9 select_reduce_fusion.table_two
  4.1 0.9 select_reduce_fusion.1.table_one
  5.0 155.9 %shard_map.130 = (bf16[16,12288]{1,0:T(8,128)(2,1)}, bf16[288,16,128]{2,1,0:T(8,128)(2,1)}, bf16[288,16,128]{2,1,0:T(8,128)(2,1)}, bf16[8,16,16,1536]{3,2,1,0:T(8,128)(2,1)}, bf16[4,16,16,3072]{3,2,1,0:T(8,128)(2,1)}) custom-call(s32[1152]{0:T(1024)} %select_reduce_fusion.1.table_one, s32[1152]{0:T(1024)} %select_reduce_fusion.table_two, ...), custom_call_target="tpu_custom_call" | custom-call | tf_op jit(solution)/shard_map/pallas_call | solution.py:485
  160.8 1.8 %copy.19 = bf16[16,12288]{1,0:T(8,128)(2,1)} copy(bf16[16,12288]{1,0:T(8,128)(2,1)} %get-tuple-element.18) | data formatting | bytes 786432
  162.6 0.0 copy-start
  162.6 2.6 %copy.20 = bf16[288,16,128]{2,1,0:T(8,128)(2,1)} copy(bf16[288,16,128]{2,1,0:T(8,128)(2,1)} %get-tuple-element.19) | data formatting | bytes 2359296
  165.2 0.0 copy-done
  165.2 1.0 copy.21
Async XLA Ops:
  162.6 2.6 %copy-start = (bf16[288,16,128]{2,1,0:T(8,128)(2,1)S(1)}, bf16[288,16,128]{2,1,0:T(8,128)(2,1)}, u32[]{:S(2)}) copy-start(bf16[288,16,128]{2,1,0:T(8,128)(2,1)} %get-tuple-element.20) | copy-start | bytes 3538948

commit v5 on v4

--- a/solution.py
+++ b/solution.py
@@ -167,16 +167,17 @@
 
 
 class SeqGather:
-    def __init__(self, me, copies, base, slots):
+    def __init__(self, me, copies, base, slots, first, last):
         self.me, self.k, self.b, self.slots = me, copies, base, slots
+        self.span = pl.ds(first, last - first)
 
     def at(self, dx, fl):
         me = self.me
-        return self.slots.at[(me.x + dx) % 4 * 2 + (me.yl + fl) % 2]
+        return self.slots.at[(me.x + dx) % 4 * 2 + (me.yl + fl) % 2, :, self.span]
 
     def half(self, dx, fl, i):
         me = self.me
-        return self.slots.at[(me.x + dx) % 4 * 2 + (me.yl + fl) % 2, pl.ds(i * 128, 128)]
+        return self.slots.at[(me.x + dx) % 4 * 2 + (me.yl + fl) % 2, pl.ds(i * 128, 128), self.span]
 
     def start(self):
         me, k, b = self.me, self.k, self.b
@@ -237,7 +238,8 @@
     whole = TensorGather(me, k, 0, grad, lambda t: rows.at[t])
     grads = TensorGather(me, k, 15, grad_x, lambda t: grad_all.at[:, t])
     ins = TensorGather(me, k, 30, in_x, lambda t: in_all.at[:, t])
-    pre_cols = SeqGather(me, k, 45, all_pre)
+    pre_cols = SeqGather(me, k, 45, all_pre, 0, 1024)
+    end_cols = SeqGather(me, k, 84, all_pre, 1024, 1536)
     act_cols = RowGather(me, k, 80, all_acts.at[me.x], all_acts)
     whole.start()
     rows[me.t] = grad[...]
@@ -312,13 +314,14 @@
     lax.fori_loop(0, 2, pre, 0)
     grads.spread()
     lax.fori_loop(2, 4, pre, 0)
+    pre_cols.start()
     for i, (dx, fl) in enumerate(others):
         k.arrived(60 + i, in_x.at[(me.x + 4 - dx) % 4 * 2 + (me.yl + fl) % 2], me.dev(dx=-dx, fl=fl))
     mine[1].start()
     grads.middle()
     ins.start()
     lax.fori_loop(4, 6, pre, 0)
-    pre_cols.start()
+    end_cols.start()
     loads[1].start()
 
     def block_products(source, buffers, right, cuts, first_step, last_step):
@@ -353,6 +356,7 @@
     act_cols.finish()
     mine[0].wait()
     block_products(grad_all, lefts, all_acts, 4, 0, 3)
+    pre_cols.spread()
     ins.spread()
     block_products(grad_all, lefts, all_acts, 4, 3, 6)
 
@@ -365,7 +369,7 @@
 
     lax.fori_loop(0, 72, cut_two, 0)
     k.send(73, two.at[(me.yl + 1) % 2], two_got, side)
-    pre_cols.spread()
+    end_cols.spread()
     ins.middle()
     loads[1].wait()
     k.drain(settled)
@@ -385,6 +389,7 @@
 
     back(0)
     back(1)
+    pre_cols.cross()
     back(2)
     back(3)
     own = rows.at[pl.ds(me.c * 8, 8)]
@@ -404,7 +409,7 @@
     lax.fori_loop(me.z * 2, me.z * 2 + 2, add_pair, 0)
 
     ins.finish()
-    pre_cols.cross()
+    end_cols.cross()
     k.arrived(71, far_up, me.dev(dz=-1))
     own[zu * 2] = (own[zu * 2].astype(F32) + far_up[...].astype(F32)).astype(BF)
     k.send(74, own.at[pl.ds(zu * 2, 2)], near_up, me.dev(dz=1))
@@ -413,6 +418,7 @@
     k.send(75, own.at[pl.ds(zd * 2, 2)], near_down, me.dev(dz=-1))
 
     pre_cols.finish()
+    end_cols.finish()
     mine[1].wait()
     block_products(in_all, in_lefts, all_pre, 8, 0, 3)
 
@@ -489,8 +495,8 @@
         out_specs=(VMEM, VMEM, VMEM, ANY, ANY),
         scratch_shapes=[
             *[pltpu.VMEM(shape, BF) if shape else pltpu.VMEM((256, 256), F32) for shape in shapes],
-            pltpu.SemaphoreType.DMA((84,)),
-            pltpu.SemaphoreType.DMA((84,)),
+            pltpu.SemaphoreType.DMA((93,)),
+            pltpu.SemaphoreType.DMA((93,)),
             pltpu.SemaphoreType.DMA((4,)),
             pltpu.SemaphoreType.DMA((2,)),
         ],

time: 167 us -> 161 us (0.964)
  Pallas kernels: 156 us -> 151 us
    pallas_call x1, Pallas kernels: 156 us -> 151 us  [shards(): pl.pallas_call(backward, out_shape=(sds(*row), sds(288, 16, 128), sds(288...]
where the time goes in v5:
time: 161 us
  Pallas kernels  151 us (94%)
  local copies, waits for them, and re-layouts  5.37 us (3%)
  other arithmetic  3.03 us (2%)
  between operations  1.94 us (1%)
    pallas_call x1, Pallas kernels, shards(): pl.pallas_call(backward, out_shape=(sds(*row), sds(288, 16, 128), sds(288...  151 us
    unnamed x5, local copies, waits for them, and re-layouts  5.37 us

profile of v5, /device:TPU:1, one launch (start us, length us, event | category | flops | bytes accessed | tf_op | source)
XLA Modules:
  0.0 161.1 jit_solution(1582785152947398920)
XLA Ops:
  1.9 1.3 add_select_fusion
  3.2 0.9 select_reduce_fusion.table_two
  4.1 0.9 select_reduce_fusion.1.table_one
  5.0 150.8 %shard_map.130 = (bf16[16,12288]{1,0:T(8,128)(2,1)}, bf16[288,16,128]{2,1,0:T(8,128)(2,1)}, bf16[288,16,128]{2,1,0:T(8,128)(2,1)}, bf16[8,16,16,1536]{3,2,1,0:T(8,128)(2,1)}, bf16[4,16,16,3072]{3,2,1,0:T(8,128)(2,1)}) custom-call(s32[1152]{0:T(1024)} %select_reduce_fusion.1.table_one, s32[1152]{0:T(1024)} %select_reduce_fusion.table_two, ...), custom_call_target="tpu_custom_call" | custom-call | tf_op jit(solution)/shard_map/pallas_call | solution.py:491
  155.7 1.8 %copy.19 = bf16[16,12288]{1,0:T(8,128)(2,1)} copy(bf16[16,12288]{1,0:T(8,128)(2,1)} %get-tuple-element.18) | data formatting | bytes 786432
  157.5 0.0 copy-start
  157.5 2.6 %copy.20 = bf16[288,16,128]{2,1,0:T(8,128)(2,1)} copy(bf16[288,16,128]{2,1,0:T(8,128)(2,1)} %get-tuple-element.19) | data formatting | bytes 2359296
  160.1 0.0 copy-done
  160.1 1.0 copy.21
Async XLA Ops:
  157.5 2.6 %copy-start = (bf16[288,16,128]{2,1,0:T(8,128)(2,1)S(1)}, bf16[288,16,128]{2,1,0:T(8,128)(2,1)}, u32[]{:S(2)}) copy-start(bf16[288,16,128]{2,1,0:T(8,128)(2,1)} %get-tuple-element.20) | copy-start | bytes 3538948
